TPU v7x, 128 devices: a whole 4x4x4 slice. The times are simulated.
128 devices in a mesh: dp: 32 (over x, z, core), tensor: 4 (over y).
Axes of the slice: x: 4, y: 4, z: 4, core: 2. Of those that a mesh axis runs over, the one named last changes fastest.
Arguments:
- hidden: bfloat16 [4096, 4096], P('dp', 'tensor'), may hold values from -6 to 6
- grad_out: bfloat16 [4096, 4096], P('dp', 'tensor'), may hold values from -0.59765625 to 0.59765625
- routes: int32 [4096, 8], P('dp'), may hold values from 0 to 63, all different within a row; in each aligned block of 128 rows (0 to 127, 128 to 255, ...) at most 20 rows name the same one
- route_probs: float32 [4096, 8], P('dp'), may hold values from 0.02 to 0.5
- w_gate: bfloat16 [64, 4096, 1536], P('dp', None, 'tensor'), may hold values from -0.09375 to 0.09375
- w_up: bfloat16 [64, 4096, 1536], P('dp', None, 'tensor'), may hold values from -0.09375 to 0.09375
- w_down: bfloat16 [64, 1536, 4096], P('dp', 'tensor'), may hold values from -0.15625 to 0.15625
- partner: int32 [32], replicated, may hold values from 0 to 31, as said below
- swap_count: int32 [32], replicated, may hold values from 1 to 64, as said below
Outputs:
- input_grad: bfloat16 [4096, 4096], P('dp', 'tensor')
- router_grad: bfloat16 [4096, 8], P('dp')
Inputs may be any that keep to these rules, and one draw needn't show every extreme that they name: `routes`: each row names 8 different experts; within the 128 rows of one index of dp no expert is named by more than 20 rows, and in every draw some expert is named by exactly 20 rows there. A perfect matching: partner[partner[r]] = r and partner[r] != r; r and partner[r] differ in exactly one of their three lowest bits. `swap_count`: equal for both members of a matched pair; equal to 64 for some pair in every draw.
All inputs are finite; a program needn't handle non-finite values.
Results may differ from a plain program's by a relative error of at most 0.015.
Values may be sent and summed in bfloat16 or wider, within the bound.
A program may use at most 192 MiB of HBM per device.

v0:
```python
import jax
import jax.numpy as jnp
from jax import lax
from jax.sharding import PartitionSpec as P


def swapped(block, axis, apart):
    count = lax.axis_size(axis)
    route = []
    for low in range(count):
        high = low | 1 << apart
        if high != low and high < count:
            route += [(low, high), (high, low)]
    return lax.ppermute(block, axis, route)


def local(hidden, grad_out, routes, route_probs, w_gate, w_up, w_down, partner, swap_count):
    tok_rows, quarter = hidden.shape
    top_count = routes.shape[1]
    local_experts = w_gate.shape[0]
    rank_count = lax.axis_size("dp")
    experts = local_experts * rank_count
    capacity = tok_rows * top_count * 5 // (4 * experts)
    flat_routes = routes.reshape(-1)
    onehot = (flat_routes[:, None] == jnp.arange(experts, dtype=jnp.int32)[None, :]).astype(
        jnp.int32
    )
    before = jnp.cumsum(onehot, axis=0) - onehot
    position = jnp.sum(before * onehot, axis=1)
    slot_index = flat_routes * capacity + position
    pair_owner = jnp.arange(tok_rows * top_count, dtype=jnp.int32) // top_count
    slot_owner = jnp.zeros((experts * capacity,), jnp.int32).at[slot_index].set(pair_owner)
    slot_live = jnp.zeros((experts * capacity,), jnp.bfloat16).at[slot_index].set(1.0)[:, None]
    whole_in, whole_cot = (
        lax.all_gather(hidden, "tensor", axis=1, tiled=True),
        lax.all_gather(grad_out, "tensor", axis=1, tiled=True),
    )
    send_in = (whole_in[slot_owner] * slot_live).reshape(rank_count, local_experts * capacity, -1)
    send_cot = (whole_cot[slot_owner] * slot_live).reshape(rank_count, local_experts * capacity, -1)
    expert_in, expert_cot = (
        lax.all_to_all(send_in, "dp", split_axis=0, concat_axis=0, tiled=True),
        lax.all_to_all(send_cot, "dp", split_axis=0, concat_axis=0, tiled=True),
    )
    width = expert_in.shape[2]
    expert_in = expert_in.reshape(rank_count, local_experts, capacity, width)
    expert_cot = expert_cot.reshape(rank_count, local_experts, capacity, width)
    gate_pre = jnp.einsum("slcd,ldf->slcf", expert_in, w_gate, preferred_element_type=jnp.float32)
    up_pre = jnp.einsum("slcd,ldf->slcf", expert_in, w_up, preferred_element_type=jnp.float32)
    back_grad = jnp.einsum("slcd,lfd->slcf", expert_cot, w_down, preferred_element_type=jnp.float32)
    sigmoid_gate = jax.nn.sigmoid(gate_pre)
    act = gate_pre * sigmoid_gate
    prob_partial = jnp.sum(back_grad * act * up_pre, axis=3)
    gate_grad = (
        back_grad * up_pre * sigmoid_gate * (1.0 + gate_pre * (1.0 - sigmoid_gate))
    ).astype(jnp.bfloat16)
    up_grad = (back_grad * act).astype(jnp.bfloat16)
    slot_partial = jnp.einsum(
        "slcf,ldf->slcd", gate_grad, w_gate, preferred_element_type=jnp.float32
    )
    slot_partial = slot_partial + jnp.einsum(
        "slcf,ldf->slcd", up_grad, w_up, preferred_element_type=jnp.float32
    )
    slot_grad = lax.psum_scatter(
        slot_partial.astype(jnp.bfloat16), "tensor", scatter_dimension=3, tiled=True
    )
    slot_prob = lax.psum(prob_partial, "tensor").astype(jnp.bfloat16)
    back_slots, back_probs = (
        lax.all_to_all(slot_grad, "dp", split_axis=0, concat_axis=0, tiled=True),
        lax.all_to_all(slot_prob, "dp", split_axis=0, concat_axis=0, tiled=True),
    )
    gathered = back_slots.reshape(experts * capacity, quarter)[slot_index].reshape(
        tok_rows, top_count, quarter
    )
    owner_grad = jnp.sum(route_probs[:, :, None] * gathered, axis=1).astype(jnp.bfloat16)
    router_grad = back_probs.reshape(experts * capacity)[slot_index].reshape(tok_rows, top_count)
    own_rank = lax.axis_index("dp")
    partner_rank = partner[own_rank]
    live_swap = swap_count[own_rank]
    swap_rows = tok_rows // 2
    tail_rows = owner_grad[tok_rows - swap_rows :]
    incoming = tail_rows
    for bit_number in range(min(3, rank_count.bit_length() - 1)):
        received = swapped(tail_rows, "dp", bit_number)
        incoming = jnp.where(
            partner_rank == jnp.bitwise_xor(own_rank, 1 << bit_number), received, incoming
        )
    row_number = jnp.arange(swap_rows, dtype=jnp.int32) + (tok_rows - swap_rows)
    taken = (row_number >= tok_rows - live_swap)[:, None]
    kept_tail = jnp.where(taken, incoming, tail_rows)
    input_grad = jnp.concatenate([owner_grad[: tok_rows - swap_rows], kept_tail], axis=0)
    return (input_grad, router_grad)


def solution(mesh):
    placed = (
        P("dp", "tensor"),
        P("dp", "tensor"),
        P("dp", None),
        P("dp", None),
        P("dp", None, "tensor"),
        P("dp", None, "tensor"),
        P("dp", "tensor", None),
        P(),
        P(),
    )
    return jax.shard_map(
        local,
        mesh=mesh,
        in_specs=placed,
        out_specs=(P("dp", "tensor"), P("dp", None)),
        check_vma=False,
    )
```

profile of v0, /device:TPU:0, one launch (start us, length us, event | category | flops | bytes accessed | tf_op | source)
XLA Modules:
  0.0 659.3 jit_solution(7280975755395638405)
XLA Ops:
  7.2 0.7 all-gather.5.cloned.1.call-update
  7.9 0.7 all-gather.3.cloned.1.call-update
  8.6 0.8 copy.50
  9.6 18.0 %reduce-window.6 = s32[64,8,128]{2,1,0:T(8,128)S(1)} reduce-window(s32[64,8,128]{2,1,0:T(8,128)S(1)} %fusion.26, s32[]{:T(128)} %constant.19.clone.1), window={size=1x1x128 pad=0_0x0_0x127_0}, to_apply=%region_0.0 | reduce-window | flops 8323072 | bytes 524292 | tf_op jit(solution)/shard_map/reduce-window
  27.7 0.1 slice.24
  27.8 0.1 copy.52
  28.1 0.7 broadcast_multiply_fusion.2
  28.8 0.1 copy.49
  28.9 0.1 mul.70
  29.0 0.1 broadcast_add_fusion
  29.2 4.3 scatter_custom_fusion
  33.5 7.9 %scatter_custom_fusion.1 = bf16[1280]{0:T(1024)(128)(2,1)S(1)} fusion(s32[1024]{0:T(1024)S(1)} %bitcast.111, bf16[1024]{0:T(1024)(128)(2,1)S(1)} %broadcast.85, bf16[]{:T(256)} %constant.46.clone.1), kind=kCustom, calls=%fused_computation.60 | custom fusion | bytes 2562 | tf_op jit(solution)/shard_map/scatter | solution.py:33
  41.6 20.0 %gather_fusion.1 = bf16[1280,4096]{1,0:T(8,128)(2,1)} fusion(bf16[128,4096]{1,0:T(8,128)(2,1)} %all-gather.5.cloned.1.call-done, s32[2048]{0:T(1024)S(1)} %pad_clamp_fusion), kind=kCustom, calls=%fused_computation.1 | custom fusion | bytes 20976640 | tf_op jit(solution)/shard_map/gather | solution.py:38
  61.6 0.7 all-gather.3.cloned.1.call-done
  62.4 20.1 %gather_fusion = bf16[1280,4096]{1,0:T(8,128)(2,1)} fusion(bf16[128,4096]{1,0:T(8,128)(2,1)} %all-gather.3.cloned.1.call-done, s32[2048]{0:T(1024)S(1)} %pad_clamp_fusion), kind=kCustom, calls=%fused_computation | custom fusion | bytes 20976640 | tf_op jit(solution)/shard_map/gather | solution.py:39
  82.4 12.4 %broadcast_multiply_fusion.1 = (bf16[32,40,4096]{2,1,0:T(8,128)(2,1)}, bf16[32,40,4096]{2,1,0:T(8,128)(2,1)S(1)}) fusion(bf16[32,40,4096]{2,1,0:T(8,128)(2,1)} %bitcast.103, bf16[32,40]{1,0:T(8,128)(2,1)S(1)} %mul.72, bf16[32,40,4096]{2,1,0:T(8,128)(2,1)} %bitcast.102), kind=kLoop, calls=%fused_computation.18 | loop fusion | flops 10485760 | bytes 41945600 | tf_op jit(solution)/shard_map/mul | solution.py:39
  94.9 125.3 %all_to_all.20 = bf16[32,40,4096]{2,1,0:T(8,128)(2,1)} all-to-all(bf16[32,40,4096]{2,1,0:T(8,128)(2,1)S(1)} %get-tuple-element.13), channel_id=1, replica_groups=mesh['dp'=32,'tensor'=4] {'dp'}, dimensions={0} | all-to-all | bytes 20971520 | tf_op jit(solution)/shard_map/all_to_all | solution.py:41
  220.2 5.0 all-to-all-start
  225.2 0.6 reduce-scatter.2.cloned.1.call-start
  225.8 13.5 %copy.55 = bf16[32,40,4096]{2,0,1:T(8,128)(2,1)} copy(bf16[32,40,4096]{2,1,0:T(8,128)(2,1)} %all_to_all.20) | data formatting | bytes 20971520 | tf_op jit(solution)/shard_map/all_to_all | solution.py:41
  239.3 10.3 %fusion.3 = f32[2,32,20,384]{3,1,2,0:T(8,128)S(1)} fusion(bf16[32,2,20,4096]{3,0,2,1:T(8,128)(2,1)} %bitcast.104, bf16[2,4096,384]{2,1,0:T(8,128)(2,1)} %param.13), kind=kOutput, calls=%fused_computation.10 | convolution fusion | flops 4026531840 | bytes 18743296 | tf_op jit(solution)/shard_map/slcd,ldf->slcf/dot_general | solution.py:47
  249.6 120.3 %all-to-all-done = bf16[32,40,4096]{2,1,0:T(8,128)(2,1)} async-done(((bf16[32,40,4096]{2,1,0:T(8,128)(2,1)}), bf16[32,40,4096]{2,1,0:T(8,128)(2,1)}, u32[]{:S(2)}, u32[]{:S(2)}) %all-to-all-start) | async-done | bytes 10485792 | tf_op jit(solution)/shard_map/all_to_all | solution.py:42
  369.9 13.7 %copy.54 = bf16[32,40,4096]{2,0,1:T(8,128)(2,1)} copy(bf16[32,40,4096]{2,1,0:T(8,128)(2,1)} %all-to-all-done) | data formatting | bytes 20971520 | tf_op jit(solution)/shard_map/all_to_all | solution.py:42
  383.6 10.1 %fusion.5 = f32[2,32,20,384]{3,1,2,0:T(8,128)S(1)} fusion(bf16[32,2,20,4096]{3,0,2,1:T(8,128)(2,1)} %bitcast.106, bf16[2,384,4096]{2,1,0:T(8,128)(2,1)} %param.15), kind=kOutput, calls=%fused_computation.12 | convolution fusion | flops 4026531840 | bytes 18743296 | tf_op jit(solution)/shard_map/slcd,lfd->slcf/dot_general | solution.py:49
  393.8 11.1 %fusion.19 = (f32[32,2,20]{0,2,1:T(8,128)S(1)}, f32[2,32,20,384]{3,1,2,0:T(8,128)S(1)}) fusion(f32[2,32,20,384]{3,1,2,0:T(8,128)S(1)} %fusion.3, f32[2,32,20,384]{3,1,2,0:T(8,128)S(1)} %fusion.5, bf16[32,2,20,4096]{3,0,2,1:T(8,128)(2,1)} %bitcast.105, bf16[2,4096,384]{2,1,0:T(8,128)(2,1)} %param.14), kind=kOutput, calls=%fused_computation.34 | convolution fusion | flops 4029971200 | bytes 22680576 | tf_op jit(solution)/shard_map/slcd,ldf->slcf/dot_general | solution.py:48
  404.9 13.1 %fusion.1 = f32[2,32,20,4096]{3,1,2,0:T(8,128)} fusion(bf16[2,4096,384]{2,1,0:T(8,128)(2,1)} %param.13, f32[2,32,20,384]{3,1,2,0:T(8,128)S(1)} %fusion.3, f32[2,32,20,384]{3,1,2,0:T(8,128)S(1)} %get-tuple-element.15, f32[2,32,20,384]{3,1,2,0:T(8,128)S(1)} %fusion.5), kind=kOutput, calls=%fused_computation.8 | convolution fusion | flops 4031447040 | bytes 33161216 | tf_op jit(solution)/shard_map/slcf,ldf->slcd/dot_general | solution.py:57
  418.0 14.8 %fusion = bf16[32,2,20,4096]{3,0,2,1:T(8,128)(2,1)} fusion(f32[2,32,20,4096]{3,1,2,0:T(8,128)} %fusion.1, bf16[2,4096,384]{2,1,0:T(8,128)(2,1)} %param.14, f32[2,32,20,384]{3,1,2,0:T(8,128)S(1)} %fusion.3, f32[2,32,20,384]{3,1,2,0:T(8,128)} %copy-done), kind=kOutput, calls=%fused_computation.7 | convolution fusion | flops 4039966720 | bytes 41680896 | tf_op jit(solution)/shard_map/slcf,ldf->slcd/dot_general | solution.py:60
  432.8 118.2 %reduce-scatter.2.cloned.1.call-done = bf16[32,2,20,1024]{3,0,2,1:T(8,128)(2,1)} async-done(((bf16[32,2,20,4096]{3,0,2,1:T(8,128)(2,1)}), bf16[32,2,20,1024]{3,0,2,1:T(8,128)(2,1)}) %reduce-scatter.2.cloned.1.call-update) | async-done | bytes 2621456 | tf_op jit(solution)/shard_map/reduce_scatter | solution.py:63
  551.0 6.0 copy.56
  556.9 7.2 %all-to-all-start.2 = ((bf16[32,2,20,1024]{3,1,2,0:T(2,128)(2,1)}), bf16[32,2,20,1024]{3,1,2,0:T(2,128)(2,1)S(1)}, u32[]{:S(2)}, u32[]{:S(2)}) async-start(bf16[32,2,20,1024]{3,1,2,0:T(2,128)(2,1)} %copy.56), calls=%async_computation.3 | async-start | bytes 5242880 | tf_op jit(solution)/shard_map/all_to_all | solution.py:68
  564.2 0.1 copy.48
  564.3 34.5 %all-to-all-done.2 = bf16[32,2,20,1024]{3,1,2,0:T(2,128)(2,1)S(1)} async-done(((bf16[32,2,20,1024]{3,1,2,0:T(2,128)(2,1)}), bf16[32,2,20,1024]{3,1,2,0:T(2,128)(2,1)S(1)}, u32[]{:S(2)}, u32[]{:S(2)}) %all-to-all-start.2) | async-done | bytes 2621472 | tf_op jit(solution)/shard_map/all_to_all | solution.py:68
  598.8 2.6 copy.57
  601.4 3.6 reshape.93
  605.1 5.4 gather_fusion.2
  610.5 3.0 fusion.10
  613.4 1.0 collective-permute-start
  614.5 0.6 collective-permute-start.1
  615.1 0.6 dynamic_slice.6
  616.3 15.1 %psum.7 = bf16[32,2,20]{0,1,2:T(2,128)(2,1)S(1)} all-reduce(f32[32,2,20]{0,1,2:T(2,128)S(1)} %copy.58), channel_id=1, replica_groups=mesh['dp'=32,'tensor'=4] {'tensor'}, use_global_device_ids=true, to_apply=%region_8.9 | all-reduce | flops 1280 | bytes 7680 | tf_op jit(solution)/shard_map/psum | solution.py:66
  631.4 0.7 copy.59
  632.1 4.7 all-to-all-start.3
  636.8 0.6 dynamic_slice.7
  639.3 4.7 all-to-all-done.3
  644.1 0.1 reshape.94
  644.2 6.8 %gather_fusion.3 = bf16[1024]{0:T(1024)(128)(2,1)S(1)} fusion(bf16[1280]{0:T(1024)(128)(2,1)S(1)} %reshape.94, s32[1024]{0:T(1024)S(1)} %broadcast_clamp_fusion), kind=kCustom, calls=%fused_computation.3 | custom fusion | bytes 8192 | tf_op jit(solution)/shard_map/gather | solution.py:75
  651.1 0.7 copy.60
  651.8 0.7 pad_maximum_fusion
  (35 shorter events, 0.9 us)
Async XLA Ops:
  7.2 34.4 %all-gather.5.cloned.1.call-start = ((), (), s32[]{:S(2)}) async-start(), calls=%async_computation.6 | async-start | bytes 1310720 | tf_op jit(solution)/shard_map/all_gather | solution.py:35
  7.9 54.5 %all-gather.3.cloned.1.call-start = ((), (), s32[]{:S(2)}) async-start(), calls=%async_computation.5 | async-start | bytes 1310720 | tf_op jit(solution)/shard_map/all_gather | solution.py:36
  220.2 149.7 %all-to-all-start = ((bf16[32,40,4096]{2,1,0:T(8,128)(2,1)}), bf16[32,40,4096]{2,1,0:T(8,128)(2,1)}, u32[]{:S(2)}, u32[]{:S(2)}) async-start(bf16[32,40,4096]{2,1,0:T(8,128)(2,1)} %get-tuple-element.12), calls=%async_computation | async-start | bytes 20971520 | tf_op jit(solution)/shard_map/all_to_all | solution.py:42
  225.2 325.8 %reduce-scatter.2.cloned.1.call-start = ((), (), s32[]{:S(2)}) async-start(), calls=%async_computation.7 | async-start | bytes 13107200 | tf_op jit(solution)/shard_map/reduce_scatter | solution.py:63
  393.8 11.1 %copy-start = (f32[2,32,20,384]{3,1,2,0:T(8,128)}, f32[2,32,20,384]{3,1,2,0:T(8,128)S(1)}, u32[]{:S(2)}) copy-start(f32[2,32,20,384]{3,1,2,0:T(8,128)S(1)} %fusion.5) | copy-start | bytes 5898244
  432.8 131.4 %copy-start.1 = (f32[128,8]{0,1:T(8,128)S(1)}, f32[128,8]{0,1:T(8,128)}, u32[]{:S(2)}) copy-start(f32[128,8]{0,1:T(8,128)} %param.12) | copy-start | bytes 12292
  556.9 41.9 %all-to-all-start.2 = ((bf16[32,2,20,1024]{3,1,2,0:T(2,128)(2,1)}), bf16[32,2,20,1024]{3,1,2,0:T(2,128)(2,1)S(1)}, u32[]{:S(2)}, u32[]{:S(2)}) async-start(bf16[32,2,20,1024]{3,1,2,0:T(2,128)(2,1)} %copy.56), calls=%async_computation.3 | async-start | bytes 5242880 | tf_op jit(solution)/shard_map/all_to_all | solution.py:68
  605.1 10.0 %copy-start.2 = (s32[32]{0:T(128)S(1)}, s32[32]{0:T(128)}, u32[]{:S(2)}) copy-start(s32[32]{0:T(128)} %param.17) | copy-start | bytes 388
  605.1 31.7 %copy-start.3 = (s32[32]{0:T(128)S(1)}, s32[32]{0:T(128)}, u32[]{:S(2)}) copy-start(s32[32]{0:T(128)} %param.16) | copy-start | bytes 388
  613.4 38.3 %collective-permute-start = (bf16[64,1024]{1,0:T(8,128)(2,1)S(1)}, bf16[64,1024]{1,0:T(8,128)(2,1)S(1)}, u32[]{:S(2)}, u32[]{:S(2)}) collective-permute-start(bf16[64,1024]{1,0:T(8,128)(2,1)S(1)} %get-tuple-element.11), channel_id=1, source_target_pairs={{0,16},{16,0},{4,20},{20,4},{8,24},{24,8},{12,28},{28,12},{32,48},... | collective-permute-start | bytes 393224 | tf_op jit(solution)/shard_map/ppermute | solution.py:14
  614.5 37.3 %collective-permute-start.1 = (bf16[64,1024]{1,0:T(8,128)(2,1)S(1)}, bf16[64,1024]{1,0:T(8,128)(2,1)S(1)}, u32[]{:S(2)}, u32[]{:S(2)}) collective-permute-start(bf16[64,1024]{1,0:T(8,128)(2,1)S(1)} %get-tuple-element.11), channel_id=1, source_target_pairs={{0,8},{8,0},{4,12},{12,4},{16,24},{24,16},{20,28},{28,20},{32,40},... | collective-permute-start | bytes 393224 | tf_op jit(solution)/shard_map/ppermute | solution.py:14
  615.0 36.7 %collective-permute-start.2 = (bf16[64,1024]{1,0:T(8,128)(2,1)S(1)}, bf16[64,1024]{1,0:T(8,128)(2,1)S(1)}, u32[]{:S(2)}, u32[]{:S(2)}) collective-permute-start(bf16[64,1024]{1,0:T(8,128)(2,1)S(1)} %get-tuple-element.11), channel_id=1, source_target_pairs={{0,4},{4,0},{8,12},{12,8},{16,20},{20,16},{24,28},{28,24},{32,36},... | collective-permute-start | bytes 393224 | tf_op jit(solution)/shard_map/ppermute | solution.py:14
  632.1 11.9 %all-to-all-start.3 = ((bf16[32,2,20]{2,1,0:T(2,128)(2,1)}), bf16[32,2,20]{2,1,0:T(2,128)(2,1)S(1)}, u32[]{:S(2)}, u32[]{:S(2)}) async-start(bf16[32,2,20]{2,1,0:T(2,128)(2,1)} %copy.59), calls=%async_computation.4 | async-start | bytes 32768 | tf_op jit(solution)/shard_map/all_to_all | solution.py:69
Sparse Core Ops, SparseCore 0:
  9.7 26.4 all-gather.4
  37.9 24.4 all-gather.2
  432.9 118.0 reduce-scatter.1
where the time goes:
time: 665 us; the launch traced here: 659 us
  waiting for transfers between devices  280 us (42%)
  blocking collectives  140 us (21%)
  local copies, waits for them, and re-layouts  108 us (16%)
  matrix products  59.4 us (9%)
  other arithmetic  35.2 us (5%)
  starting transfers between devices  19.1 us (3%)
  between operations  16.9 us (3%)
    all_to_all x1, blocking collectives, local(): lax.all_to_all(send_in, 'dp', split_axis=0, concat_axis=0, tiled=True)  125 us
    all_to_all x1, waiting for transfers between devices, local(): lax.all_to_all(send_cot, 'dp', split_axis=0, concat_axis=0, tiled=True)  120 us
    reduce_scatter x1, waiting for transfers between devices, local(): lax.psum_scatter(slot_partial.astype(jnp.bfloat16), 'tensor', scatter_dim...  118 us
    all_to_all x1, waiting for transfers between devices, local(): lax.all_to_all(slot_grad, 'dp', split_axis=0, concat_axis=0, tiled=True)  34.5 us
    gather x1, local copies, waits for them, and re-layouts, local(): whole_cot[slot_owner] * slot_live  20.1 us
    gather x1, local copies, waits for them, and re-layouts, local(): whole_in[slot_owner] * slot_live  20 us
    another operation x3, other arithmetic  18.2 us
    psum x1, blocking collectives, local(): slot_prob = lax.psum(prob_partial, 'tensor').astype(jnp.bfloat16)  15.1 us
  transfers between devices with their start and end apart: 9, of which 5 were waited for; matrix products, arithmetic and copies ran while one was open for 13% of the time, Pallas kernels for 0%

commit v1 on v0

v1 whole, which is shorter than its diff:
```python
import functools
import jax
import jax.numpy as jnp
from jax import lax
from jax.experimental import pallas as pl
from jax.experimental.pallas import tpu as pltpu
from jax.sharding import PartitionSpec as P

MESH = pl.DeviceIdType.MESH
BF=jnp.bfloat16; F32=jnp.float32
OROWS=144
HA=640
GA=512
CA=HA+GA
CQ=2048-CA
STEPS=(0,-1,1,2)
CHIPS=((0,0),(0,-1),(-1,0),(-1,-1),(0,1),(1,0),(-1,1),(1,-1),(1,1),(0,2),(2,0),(-1,2),(2,-1),(1,2),(2,1),(2,2))
PR=48
ORDERS=(("x","y","z"),("y","z","x"),("z","x","y"))
JS=(2,1,-1,0)

def nt(a,b): return lax.dot_general(a,b,(((1,),(1,)),((),())),preferred_element_type=F32)
def nn(a,b): return jnp.dot(a,b,preferred_element_type=F32)

def expert_kernel(hid, gra, ext, wg_hbm, wu_hbm, wd_hbm, D, gq, wg, wu, wd, xh, xg, ga, ex, rs, rr, onehot, prob, sprob, qb,
                  gate, up, back, gg, ug, spt, own_sem, wsem, qsem, dsem, send_sem, recv_sem):
    dp = lax.axis_index("dp"); y = lax.axis_index("tensor")
    x = dp // 8; z = (dp // 2) % 4; c = dp % 2
    here = {"x": x, "y": y, "z": z}
    def device(axis, step):
        if axis == "c":
            return {"dp": x * 8 + z * 2 + (1 - c), "tensor": y}
        at = dict(here)
        at[axis] = (at[axis] + step + 4) % 4
        return {"dp": at["x"] * 8 + at["z"] * 2 + c, "tensor": at["y"]}
    barrier = pltpu.get_barrier_semaphore()
    partners = [device(a, s) for a in "xyz" for s in (1, -1)] + [device("c", 0)]
    for p in partners:
        pl.semaphore_signal(barrier, inc=1, device_id=p, device_id_type=MESH)
    pl.semaphore_wait(barrier, len(partners))

    number = [0]
    pending = []
    def send(src, dst, to):
        n = number[0]; number[0] += 1
        copy = pltpu.make_async_remote_copy(src_ref=src, dst_ref=dst, send_sem=send_sem.at[n],
            recv_sem=recv_sem.at[n], device_id=to, device_id_type=MESH)
        copy.start()
        pending.append(copy)
        return copy
    mine = [pltpu.make_async_copy(a, b, own_sem.at[i]) for i, (a, b) in enumerate((
        (ext, ex.at[x, z, c]),
        (hid.at[:, pl.ds(0, HA)], ga.at[x, z, c, :, pl.ds(0, HA)]),
        (gra.at[:, pl.ds(0, GA)], ga.at[x, z, c, :, pl.ds(HA, GA)]),
        (hid.at[:, pl.ds(HA, 1024 - HA)], gq.at[x, z, c, y, :, pl.ds(0, 1024 - HA)]),
        (gra.at[:, pl.ds(GA, 1024 - GA)], gq.at[x, z, c, y, :, pl.ds(1024 - HA, 1024 - GA)])))]
    for m in mine: m.start()
    for m in mine: m.wait()

    def view(fam, at, part="all"):
        xx = pl.ds(0, 4) if at["x"] is None else at["x"]
        if fam == "E":
            return ex.at[xx, at["z"], c]
        if fam in ("alo", "ahi"):
            first = 0 if fam == "alo" else 64
            first, count = {"all": (first, 64), "up": (first, 32), "down": (first + 32, 32)}[part]
            return ga.at[xx, at["z"], c, pl.ds(first, count)]
        if fam in ("qlo", "qhi"):
            ys = {"all": pl.ds(0, 4), "up": pl.ds(0, 2), "down": pl.ds(2, 2)}[part]
            return gq.at[xx, at["z"], c, ys, pl.ds(0 if fam == "qlo" else 64, 64)]
        rows = {"all": (0, 128), "up": (0, 64), "down": (64, 64)}[part]
        return gq.at[x, z, c, at["y"], pl.ds(*rows)]
    sibs = {}
    def to_sibling(fam, at, key):
        if key is None: return
        v = view(fam, at)
        sibs[(fam,) + key] = send(v, v, device("c", 0))
    def moved(at, axis, step):
        q = dict(at); q[axis] = (here[axis] + step + 4) % 4
        return q
    class Ring:
        def __init__(self, fam, axis, at, off):
            self.fam, self.axis, self.at, self.off = fam, axis, at, off
            v = view(fam, at)
            self.up = send(v, v, device(axis, 1))
            self.down = send(v, v, device(axis, -1))
        def key(self, step):
            if self.off is None: return None
            o = dict(self.off); o[self.axis] = step
            return (o["x"], o["z"])
        def forward(self):
            f, a = self.fam, self.axis
            before, after = moved(self.at, a, -1), moved(self.at, a, 1)
            self.up.wait_recv()
            v = view(f, before, "up")
            self.up2 = send(v, v, device(a, 1))
            to_sibling(f, before, self.key(-1))
            self.down.wait_recv()
            self.down2 = None
            if f != "E":
                v = view(f, after, "down")
                self.down2 = send(v, v, device(a, -1))
            to_sibling(f, after, self.key(1))
        def finish(self):
            self.up2.wait_recv()
            if self.down2 is not None: self.down2.wait_recv()
            to_sibling(self.fam, moved(self.at, self.axis, 2), self.key(2))
    def sets(q):
        return ((q + "lo", "x", "z"), (q + "hi", "z", "x"))
    R = {}
    zero = {"x": 0, "z": 0}
    def stage_one(q):
        for f, a, b in sets(q): R[f, 1] = Ring(f, a, here, zero)
        for f, a, b in sets(q): R[f, 2, 0] = Ring(f, b, here, zero)
        for f, a, b in sets(q): to_sibling(f, here, (0, 0))
    def stage_two(q, steps):
        for f, a, b in sets(q):
            for s in steps:
                off = dict(zero); off[a] = s
                R[f, 2, s] = Ring(f, b, moved(here, a, s), off)
    def forward(q, *which):
        for f, a, b in sets(q): R[(f,) + which].forward()
    def finish(q, *which):
        for f, a, b in sets(q): R[(f,) + which].finish()

    e1 = Ring("E", "x", here, zero)
    qy = Ring("Q", "y", here, None)
    stage_one("a")
    to_sibling("E", here, (0, 0))
    weights = [pltpu.make_async_copy(a, b, wsem.at[i]) for i,(a,b) in enumerate(((wg_hbm,wg),(wu_hbm,wu),(wd_hbm,wd)))]
    e1.forward()
    forward("a", 1)
    stage_two("a", (-1, 1))
    e1.finish()
    def e_sib(step):
        at = moved(here, "z", step); at["x"] = None
        v = view("E", at)
        sibs["E", "col", step] = send(v, v, device("c", 0))
    col = dict(here); col["x"] = None
    e2 = Ring("E", "z", col, None)
    finish("a", 1)
    stage_two("a", (2,))
    qy.forward()
    e2.forward()
    e_sib(-1); e_sib(1)
    forward("a", 2, 0)
    qy.finish()
    stage_one("q")
    e2.finish()
    e_sib(2)
    for w in weights: w.start()
    for k in ((0, 0), (-1, 0), (1, 0), (2, 0)): sibs[("E",) + k].wait_recv()
    for s in (-1, 1, 2): sibs["E", "col", s].wait_recv()

    place = [((x + dx + 4) % 4, (z + dz + 4) % 4) for dx, dz in CHIPS]
    for n, (px, pz) in enumerate(place):
        for s in range(2):
            block = ex[px, pz, s].astype(F32)
            for q in range(3):
                rs[q, 2 * n + s:2 * n + s + 1, :] = block[q:q + 1]
    routes = [rs[0, :, k * 128:(k + 1) * 128] for k in range(8)]
    probs = [rs[1, :, k * 128:(k + 1) * 128] + rs[2, :, k * 128:(k + 1) * 128] for k in range(8)]
    tri = (lax.broadcasted_iota(jnp.int32, (128, 128), 0) < lax.broadcasted_iota(jnp.int32, (128, 128), 1)).astype(F32).astype(BF)
    for e in range(2):
        name = (dp * 2 + e).astype(F32)
        member = jnp.zeros((32, 128), F32); weight = jnp.zeros((32, 128), F32)
        for k in range(8):
            hit = routes[k] == name
            member = member + jnp.where(hit, 1.0, 0.0)
            weight = weight + jnp.where(hit, probs[k], 0.0)
        before = nn(member.astype(BF), tri)
        offset = ((lax.broadcasted_iota(jnp.int32, (32, 128), 0) % 4) * 20).astype(F32)
        target = jnp.where(member > 0.5, before + offset, -1.0)
        for g in range(8):
            t4 = jnp.concatenate([target[g * 4 + i:g * 4 + i + 1] for i in range(4)], axis=1)
            w4 = jnp.concatenate([weight[g * 4 + i:g * 4 + i + 1] for i in range(4)], axis=1)
            oh = jnp.where(lax.broadcasted_iota(jnp.int32, (80, 512), 0).astype(F32) == t4, 1.0, 0.0)
            onehot[g, e * 80:(e + 1) * 80, :] = oh.astype(BF)
            prob[e, g * 80:(g + 1) * 80, :] = jnp.broadcast_to(jnp.sum(oh * w4, axis=1, keepdims=True), (80, 128))

    waited = set()
    def need(q, g):
        for key in CHIPS[2 * g:2 * g + 2]:
            for f, a, b in sets(q):
                if (f, key) not in waited:
                    waited.add((f, key))
                    sibs[(f,) + key].wait_recv()
    base = pl.multiple_of(y * 1024, 1024)
    def pack_own(g):
        need("a", g)
        v = jnp.concatenate([ga[px, pz].reshape(256, CA) for px, pz in place[2 * g:2 * g + 2]], axis=0)
        out = nn(onehot[g], v).astype(BF)
        rows = pl.ds(g * 80, 80)
        for e in range(2):
            xh[e, rows, pl.ds(base, HA)] = out[e * 80:(e + 1) * 80, :HA]
            xg[e, rows, pl.ds(base, GA)] = out[e * 80:(e + 1) * 80, HA:]
    class Slots:
        def __init__(self, g):
            self.g = g
            self.up = [send(v, v, device("y", 1)) for v in self.refs(y)]
            self.down = [send(v, v, device("y", -1)) for v in self.refs(y)]
        def refs(self, yy, es=pl.ds(0, 2)):
            at = pl.multiple_of(yy * 1024, 1024)
            rows = pl.ds(self.g * 80, 80)
            return xh.at[es, rows, pl.ds(at, HA)], xg.at[es, rows, pl.ds(at, GA)]
        def forward(self):
            for w in self.up: w.wait_recv()
            self.up2 = [send(v, v, device("y", 1)) for v in self.refs((y + 3) % 4, pl.ds(0, 1))]
            for w in self.down: w.wait_recv()
            self.down2 = [send(v, v, device("y", -1)) for v in self.refs((y + 1) % 4, pl.ds(1, 1))]
        def finish(self):
            for w in self.up2 + self.down2: w.wait_recv()
            for w in self.up + self.down + self.up2 + self.down2:
                w.wait_send()
                pending[:] = [q for q in pending if q is not w]
    def q_copies(g, yy):
        return [pltpu.make_async_copy(gq.at[px, pz, :, yy], qb.at[yy, i], qsem.at[yy, i])
                for i, (px, pz) in enumerate(place[2 * g:2 * g + 2])]
    def q_start(g):
        for yy in range(4):
            for w in q_copies(g, yy): w.start()
    def pack_rest(groups):
        for g in groups: need("q", g)
        q_start(groups[0])
        for g, after in zip(groups, groups[1:] + (None,)):
            for yy in range(4):
                for w in q_copies(g, yy): w.wait()
                out = nn(onehot[g], qb[yy].reshape(512, CQ)).astype(BF)
                rows = pl.ds(g * 80, 80)
                for e in range(2):
                    xh[e, rows, yy * 1024 + HA:(yy + 1) * 1024] = out[e * 80:(e + 1) * 80, :1024 - HA]
                    xg[e, rows, yy * 1024 + GA:(yy + 1) * 1024] = out[e * 80:(e + 1) * 80, 1024 - HA:]
                if after is not None:
                    for w in q_copies(after, yy): w.start()
    def hidden_units(h, e):
        rows = pl.ds(h * 320, 320)
        gate[...] = jnp.zeros_like(gate); up[...] = jnp.zeros_like(up); back[...] = jnp.zeros_like(back)
        @pl.loop(0, 8)
        def _(kk):
            cols = pl.ds(pl.multiple_of(kk * 512, 512), 512)
            a = xh[e, rows, cols]
            gate[...] += nn(a, wg[e, cols, :])
            up[...] += nn(a, wu[e, cols, :])
            back[...] += nt(xg[e, rows, cols], wd[e, :, cols])
        @pl.loop(0, 4)
        def _(r):
            here_rows = pl.ds(pl.multiple_of(r * 80, 16), 80)
            all_rows = pl.ds(pl.multiple_of(h * 320 + r * 80, 16), 80)
            gp = gate[here_rows, :]; u = up[here_rows, :]; b = back[here_rows, :]
            sig = 1.0 / (1.0 + jnp.exp(-gp))
            act = gp * sig
            sprob[e, all_rows, :] = jnp.broadcast_to(jnp.sum(b * act * u, axis=1, keepdims=True), (80, 128))
            p = prob[e, all_rows, 0:1]
            gg[here_rows, :] = (b * u * sig * (1.0 + gp * (1.0 - sig)) * p).astype(BF)
            ug[here_rows, :] = (b * act * p).astype(BF)
        @pl.loop(0, 8)
        def _(kk):
            cols = pl.ds(pl.multiple_of(kk * 512, 512), 512)
            xh[e, rows, cols] = (nt(gg[...], wg[e, cols, :]) + nt(ug[...], wu[e, cols, :])).astype(BF)

    S = {}
    forward("a", 2, -1)
    pack_own(0); S[0] = Slots(0)
    pack_own(1); S[1] = Slots(1)
    forward("a", 2, 1)
    pack_own(2); S[2] = Slots(2)
    pack_own(3)
    forward("a", 2, 2)
    for s in STEPS: finish("a", 2, s)
    for g in range(4, 8): pack_own(g)
    S[0].forward(); S[3] = Slots(3)
    S[1].forward(); S[4] = Slots(4)
    forward("q", 1)
    stage_two("q", (-1, 1))
    S[2].forward(); S[5] = Slots(5)
    forward("q", 2, 0)
    finish("q", 1)
    stage_two("q", (2,))
    S[3].forward(); S[6] = Slots(6)
    forward("q", 2, -1)
    pack_rest((0, 1))
    S[4].forward(); S[7] = Slots(7)
    forward("q", 2, 1)
    pack_rest((2, 3))
    for w in weights: w.wait()
    for g in range(4): S[g].finish()
    hidden_units(0, 0)
    S[5].forward()
    finish("q", 2, 0)
    forward("q", 2, 2)
    hidden_units(0, 1)
    S[6].forward()
    finish("q", 2, -1)
    finish("q", 2, 1)
    S[7].forward()
    finish("q", 2, 2)
    pack_rest((4, 5, 6, 7))
    for g in range(4, 8): S[g].finish()
    for e in range(2): hidden_units(1, e)
    for s in pending: s.wait_send()

    for g in range(8):
        for e in range(2):
            oh = onehot[g, e * 80:(e + 1) * 80, :].astype(F32)
            row = jnp.sum(oh * sprob[e, g * 80:(g + 1) * 80, 0:1], axis=0, keepdims=True)
            for i in range(4):
                spt[e, g * 4 + i:g * 4 + i + 1, :] = row[:, i * 128:(i + 1) * 128]
    n0 = (dp * 2).astype(F32)
    first = lax.broadcasted_iota(jnp.int32, (32, 16, 128), 1) == 0
    for k in range(8):
        r = rs[0, :, k * 128:(k + 1) * 128]
        v = jnp.where(r == n0, spt[0], 0.0) + jnp.where(r == n0 + 1.0, spt[1], 0.0)
        rr[:, :, k * 128:(k + 1) * 128] = jnp.where(first, v[:, None, :], 0.0).astype(BF)

    def d_copies(g, t):
        s = t % 2
        return [pltpu.make_async_copy(xg.at[s, pl.ds(i * OROWS, OROWS), pl.ds(0, 1024)],
                    D.at[t, place[2 * g + i // 2][0], place[2 * g + i // 2][1], i % 2], dsem.at[s, i]) for i in range(4)]
    for g in range(8):
        oht = onehot[g].astype(F32).T.astype(BF)
        for t in range(4):
            n = g * 4 + t
            if n >= 2:
                for w in d_copies((n - 2) // 4, (n - 2) % 4): w.wait()
            v = jnp.concatenate([xh[e, g * 80:(g + 1) * 80, t * 1024:(t + 1) * 1024] for e in range(2)], axis=0)
            out = nn(oht, v).astype(BF)
            for i in range(4):
                xg[t % 2, i * OROWS:i * OROWS + 128, 0:1024] = out[i * 128:(i + 1) * 128]
                xg[t % 2, i * OROWS + 128:(i + 1) * OROWS, 0:1024] = rr[g * 4 + i]
            for w in d_copies(g, t): w.start()
    for n in (30, 31):
        for w in d_copies(n // 4, n % 4): w.wait()

def experts(hid, gra, ext, wg, wu, wd):
    V=pltpu.VMEM
    A=pl.BlockSpec(memory_space=pl.ANY)
    N=4 + 3 + 7 + 4 + 2 * (40 + 32) + 64
    return pl.pallas_call(expert_kernel,
        out_shape=(jax.ShapeDtypeStruct((4,4,4,2,OROWS,1024),BF), jax.ShapeDtypeStruct((4,4,2,4,128,CQ),BF)),
        in_specs=[A]*6, out_specs=(A,A),
        scratch_shapes=[V((2,4096,384),BF),V((2,4096,384),BF),V((2,384,4096),BF),
            V((2,640,4096),BF),V((2,640,4096),BF),V((4,4,2,128,CA),BF),V((4,4,2,16,1024),BF),V((3,32,1024),F32),V((32,16,1024),BF),
            V((8,160,512),BF),V((2,640,128),F32),V((2,640,128),F32),V((4,2,2,128,CQ),BF),
            V((320,384),F32),V((320,384),F32),V((320,384),F32),V((320,384),BF),V((320,384),BF),V((2,32,128),F32),
            pltpu.SemaphoreType.DMA((5,)),pltpu.SemaphoreType.DMA((3,)),pltpu.SemaphoreType.DMA((4,2)),pltpu.SemaphoreType.DMA((2,4)),
            pltpu.SemaphoreType.DMA((N,)),pltpu.SemaphoreType.DMA((N,))],
        compiler_params=pltpu.CompilerParams(collective_id=0, has_side_effects=True, vmem_limit_bytes=63*1024*1024),
    )(hid, gra, ext, wg, wu, wd)[0]

def return_kernel(D, pick, grad, router, sib, own, r1, r2, r3, m2, m3, fin, inc, own_sem, send_sem, recv_sem):
    dp = lax.axis_index("dp"); y = lax.axis_index("tensor")
    x = dp // 8; z = (dp // 2) % 4; c = dp % 2
    here = {"x": x, "y": y, "z": z}
    def device(axis, step):
        if axis == "c":
            return {"dp": x * 8 + z * 2 + (1 - c), "tensor": y}
        at = dict(here)
        at[axis] = (at[axis] + step + 4) % 4
        return {"dp": at["x"] * 8 + at["z"] * 2 + c, "tensor": at["y"]}
    mates = []
    for bit in range(3):
        low = (dp // (1 << bit)) % 2
        mates.append({"dp": dp + (1 - 2 * low) * (1 << bit), "tensor": y})
    barrier = pltpu.get_barrier_semaphore()
    partners = [device(a, s) for a in "xyz" for s in (1, -1)] + mates
    for p in partners:
        pl.semaphore_signal(barrier, inc=1, device_id=p, device_id_type=MESH)
    pl.semaphore_wait(barrier, len(partners))

    number = [0]
    pending = []
    def send(src, dst, to):
        n = number[0]; number[0] += 1
        copy = pltpu.make_async_remote_copy(src_ref=src, dst_ref=dst, send_sem=send_sem.at[n],
            recv_sem=recv_sem.at[n], device_id=to, device_id_type=MESH)
        copy.start()
        pending.append(copy)
        return copy
    def block(p, j, k, core):
        A, B, C = ORDERS[p]
        at = {A: None, B: (here[B] + j + 4) % 4, C: (here[C] + k + 4) % 4}
        idx = tuple(pl.ds(0, 4) if at[a] is None else at[a] for a in "yxz")
        return D.at[idx + (core, pl.ds(p * PR, PR))]
    order = [(p, j, k) for j in JS for k in JS for p in range(3)]
    sibs = {}
    for p, j, k in order:
        sibs[p, j, k] = send(block(p, j, k, 1 - c), sib.at[p, JS.index(j), JS.index(k)], device("c", 0))
    NB = 6
    def own_copy(n):
        p, j, k = order[n]
        return pltpu.make_async_copy(block(p, j, k, c), own.at[n % NB], own_sem.at[n % NB])
    for n in range(NB): own_copy(n).start()
    def add(dst, *terms):
        @pl.loop(0, dst.shape[0])
        def _(i):
            total = terms[0][i].astype(F32)
            for t in terms[1:]: total = total + t[i].astype(F32)
            dst[i] = total.astype(BF)
    done = [0]
    def merge(p, j, k):
        n = done[0]; done[0] += 1
        assert order[n] == (p, j, k)
        own_copy(n).wait()
        sibs[p, j, k].wait_recv()
        m = sib.at[p, JS.index(j), JS.index(k)]
        add(m, m, own.at[n % NB])
        if n + NB < len(order): own_copy(n + NB).start()
        return m
    class Ring:
        def __init__(self, axis, land):
            self.axis, self.land = axis, land
        def start(self, far):
            a = self.axis
            self.up1 = send(far.at[0:2], self.land.at[0:2], device(a, 1))
            self.down1 = send(far.at[2:4], self.land.at[2:4], device(a, -1))
        def middle(self, after, before):
            a = self.axis
            self.up1.wait_recv()
            lo = after.at[0:2]
            add(lo, lo, self.land.at[0:2])
            self.up2 = send(after, self.land.at[4:8], device(a, 1))
            self.down1.wait_recv()
            hi = before.at[2:4]
            add(hi, hi, self.land.at[2:4])
            self.down2 = send(before, self.land.at[8:12], device(a, -1))
        def finish(self, near, out):
            self.up2.wait_recv(); self.down2.wait_recv()
            add(out, near, self.land.at[4:8], self.land.at[8:12])
    rings = {}
    M = {}
    def first(j):
        for k in JS:
            for p in range(3):
                M[p, j, k] = merge(p, j, k)
                if k == 2:
                    r = rings[p, j] = Ring(ORDERS[p][2], r1.at[p, JS.index(j)])
                    r.start(M[p, j, 2])
    def second(j):
        for p in range(3): rings[p, j].middle(M[p, j, 1], M[p, j, -1])
    def third(j):
        for p in range(3): rings[p, j].finish(M[p, j, 0], m2.at[p, JS.index(j)])
    late = {}
    first(2); first(1); second(2); first(-1); second(1); third(2)
    for p in range(3):
        late[p] = Ring(ORDERS[p][1], r2.at[p]); late[p].start(m2.at[p, 0])
    first(0); second(-1); third(1); second(0); third(-1)
    for p in range(3): late[p].middle(m2.at[p, 1], m2.at[p, 2])
    third(0)
    for p in range(3): late[p].finish(m2.at[p, 3], m3.at[p])
    last = {}
    cut = [pl.ds(0, 512), pl.ds(512, 512)]
    for p in range(3):
        A = ORDERS[p][0]
        far = m3.at[p, (here[A] + 2) % 4]
        last[p] = [send(far.at[:, cut[0]], r3.at[p, 0, :, cut[0]], device(A, 1)),
                   send(far.at[:, cut[1]], r3.at[p, 0, :, cut[1]], device(A, -1))]
    for p in range(3):
        A = ORDERS[p][0]
        for s in (0, 1):
            last[p][s].wait_recv()
            m = m3.at[p, (here[A] + (1, 3)[s]) % 4]
            m[:, cut[s]] = (m[:, cut[s]].astype(F32) + r3[p, 0, :, cut[s]].astype(F32)).astype(BF)
            last[p].append(send(m, r3.at[p, 1 + s], device(A, (1, -1)[s])))
    for p in range(3):
        A = ORDERS[p][0]
        last[p][2].wait_recv(); last[p][3].wait_recv()
        total = m3[p, here[A]].astype(F32) + r3[p, 1].astype(F32) + r3[p, 2].astype(F32)
        fin[p * PR:(p + 1) * PR, :] = total.astype(BF)
    swaps = [send(fin.at[64:128], inc.at[b], mates[b]) for b in range(3)]
    router[...] = fin[128:144, :]
    grad[0:64, :] = fin[0:64, :]
    for s in swaps: s.wait_recv()
    row = lax.broadcasted_iota(jnp.int32, (64, 1024), 0)
    kept = fin[64:128, :].astype(F32)
    taken = row >= 64 - pick[1]
    for b in range(3):
        kept = jnp.where(taken & (pick[0] == b), inc[b].astype(F32), kept)
    grad[64:128, :] = kept.astype(BF)
    for s in pending: s.wait_send()

def returned(D, pick):
    V=pltpu.VMEM
    N=48 + 3 * 4 * 4 + 3 * 4 + 3 * 4 + 3
    return pl.pallas_call(return_kernel,
        out_shape=(jax.ShapeDtypeStruct((128,1024),BF),jax.ShapeDtypeStruct((16,1024),BF)),
        in_specs=[pl.BlockSpec(memory_space=pl.ANY),pl.BlockSpec(memory_space=pltpu.SMEM)],
        out_specs=(pl.BlockSpec(memory_space=V),pl.BlockSpec(memory_space=V)),
        scratch_shapes=[V((3,4,4,4,PR,1024),BF),V((6,4,PR,1024),BF),V((3,4,12,PR,1024),BF),V((3,12,PR,1024),BF),
            V((3,3,PR,1024),BF),V((3,4,4,PR,1024),BF),V((3,4,PR,1024),BF),V((OROWS,1024),BF),V((3,64,1024),BF),
            pltpu.SemaphoreType.DMA((6,)),pltpu.SemaphoreType.DMA((N,)),pltpu.SemaphoreType.DMA((N,))],
        compiler_params=pltpu.CompilerParams(collective_id=1, has_side_effects=True, vmem_limit_bytes=62*1024*1024),
    )(D, pick)

def local(hidden, grad_out, routes, route_probs, w_gate, w_up, w_down, partner, swap_count):
    flat = route_probs.T.reshape(1, 1024)
    high = lax.reduce_precision(flat, 8, 7).astype(BF)
    low = (flat - high.astype(F32)).astype(BF)
    number = routes.T.reshape(1, 1024).astype(BF)
    ext = jnp.concatenate([number, high, low, jnp.zeros((13, 1024), BF)], axis=0)
    partial = experts(hidden, grad_out, ext, w_gate, w_up, w_down)
    rank = lax.axis_index("dp")
    apart = jnp.bitwise_xor(partner[rank], rank)
    pick = jnp.stack([apart // 2, swap_count[rank]]).astype(jnp.int32)
    grad, router = returned(partial, pick)
    return grad, router[0].reshape(8, 128).T


def solution(mesh):
    placed = (
        P("dp", "tensor"),
        P("dp", "tensor"),
        P("dp", None),
        P("dp", None),
        P("dp", None, "tensor"),
        P("dp", None, "tensor"),
        P("dp", "tensor", None),
        P(),
        P(),
    )
    return jax.shard_map(
        local,
        mesh=mesh,
        in_specs=placed,
        out_specs=(P("dp", "tensor"), P("dp", None)),
        check_vma=False,
    )
```

time: 665 us -> 296 us (0.45)
  Pallas kernels: 0 us -> 286 us
  waiting for transfers between devices: 280 us -> 0 us
  blocking collectives: 140 us -> 0 us
  local copies, waits for them, and re-layouts: 108 us -> 4.25 us
  matrix products: 59.4 us -> 0 us
  other arithmetic: 35.2 us -> 3.36 us
  starting transfers between devices: 19.1 us -> 0 us
  between operations: 16.9 us -> 1.34 us
    pallas_call x0 -> x2, Pallas kernels: none -> 286 us  [the longest x1 193 us: experts(): pl.pallas_call(expert_kernel, out_shape=(jax.ShapeDtypeStruct((4, 4, 4, 2...]
    all_to_all x3 -> x0, waiting for transfers between devices: 160 us -> none  [the longest x1 120 us: local(): lax.all_to_all(send_cot, 'dp', split_axis=0, concat_axis=0, tiled=True)]
    all_to_all x1 -> x0, blocking collectives: 125 us -> none  [local(): lax.all_to_all(send_in, 'dp', split_axis=0, concat_axis=0, tiled=True)]
    reduce_scatter x1 -> x0, waiting for transfers between devices: 118 us -> none  [local(): lax.psum_scatter(slot_partial.astype(jnp.bfloat16), 'tensor', scatter_dim...]
    dot_general x5 -> x0, matrix products: 59.4 us -> none  [the longest x1 14.8 us: local(): jnp.einsum('slcf,ldf->slcd', up_grad, w_up, preferred_element_type=jnp.fl...]
    gather x4 -> x0, local copies, waits for them, and re-layouts: 52.3 us -> none  [the longest x1 20.1 us: local(): whole_cot[slot_owner] * slot_live]
    all_to_all x3 -> x0, local copies, waits for them, and re-layouts: 29.9 us -> none  [the longest x1 13.7 us: local(): lax.all_to_all(send_cot, 'dp', split_axis=0, concat_axis=0, tiled=True)]
    another operation x3 -> x1, other arithmetic: 18.2 us -> 1.28 us  [local(): pick = jnp.stack([apart // 2, swap_count[rank]]).astype(jnp.int32)]
  transfers between devices with their start and end apart: 9 -> 0, of which waited for: 5 -> 0; matrix products, arithmetic and copies ran while one was open for 13% -> 0% of each run, Pallas kernels for 0% -> 0%
where the time goes in v1:
time: 296 us; the launch traced here: 295 us
  Pallas kernels  286 us (97%)
  local copies, waits for them, and re-layouts  4.25 us (1%)
  other arithmetic  3.36 us (1%)
    pallas_call x1, Pallas kernels, experts(): pl.pallas_call(expert_kernel, out_shape=(jax.ShapeDtypeStruct((4, 4, 4, 2...  193 us
    pallas_call x1, Pallas kernels, returned(): pl.pallas_call(return_kernel, out_shape=(jax.ShapeDtypeStruct((128, 1024)...  92.8 us

profile of v1, /device:TPU:0, one launch (start us, length us, event | category | flops | bytes accessed | tf_op | source)
XLA Modules:
  0.0 295.1 jit_solution(3969141830527691486)
XLA Ops:
  0.6 0.7 reduce-precision_convert_fusion
  1.3 0.7 convert_bitcast_fusion
  2.0 0.1 pad.5.clone
  2.1 0.7 maximum_maximum_fusion.ext
  2.8 0.0 copy-start
  2.8 0.0 copy-start.1
  2.8 193.3 %shard_map.104 = (bf16[4,4,4,2,144,1024]{5,4,3,2,1,0:T(8,128)(2,1)}, bf16[4,4,2,4,128,896]{5,4,3,2,1,0:T(8,128)(2,1)}) custom-call(bf16[128,1024]{1,0:T(8,128)(2,1)} %hid.1, bf16[128,1024]{1,0:T(8,128)(2,1)} %gra.1, bf16[16,1024]{1,0:T(8,128)(2,1)} %maximum_maximum_fusion.ext, bf16[2,4096,384]{2,1,0:T(8,128)(2,1)} %wg_hbm.1, bf16[2,4096,384]{2,1,0:T(8,128)(2,1)} %wu_hbm.1, ...), custom_call_target="tpu_custom_call" | custom-call | tf_op jit(solution)/shard_map/pallas_call | solution.py:338
  196.1 0.0 copy-done
  196.1 0.6 dynamic_slice.7
  196.7 0.0 copy-done.1
  196.7 0.6 dynamic_slice.6
  198.0 1.3 pad_add_fusion.pick
  199.3 92.8 %shard_map.105 = (bf16[128,1024]{1,0:T(8,128)(2,1)}, bf16[16,1024]{1,0:T(8,128)(2,1)}) custom-call(bf16[4,4,4,2,144,1024]{5,4,3,2,1,0:T(8,128)(2,1)} %get-tuple-element.5.D, s32[2]{0:T(128)} %pad_add_fusion.pick), custom_call_target="tpu_custom_call" | custom-call | tf_op jit(solution)/shard_map/pallas_call | solution.py:484
  292.1 1.3 slice_reduce_fusion
  293.4 1.7 copy.15
  (2 shorter events, 0.0 us)
Async XLA Ops:
  2.8 193.3 %copy-start = (s32[32]{0:T(128)S(1)}, s32[32]{0:T(128)}, u32[]{:S(2)}) copy-start(s32[32]{0:T(128)} %param.17) | copy-start | bytes 388
  2.8 193.9 %copy-start.1 = (s32[32]{0:T(128)S(1)}, s32[32]{0:T(128)}, u32[]{:S(2)}) copy-start(s32[32]{0:T(128)} %param.16) | copy-start | bytes 388

commit v2 on v1

--- a/solution.py
+++ b/solution.py
@@ -8,22 +8,20 @@
 
 MESH = pl.DeviceIdType.MESH
 BF=jnp.bfloat16; F32=jnp.float32
-OROWS=144
 HA=640
 GA=512
 CA=HA+GA
 CQ=2048-CA
 STEPS=(0,-1,1,2)
 CHIPS=((0,0),(0,-1),(-1,0),(-1,-1),(0,1),(1,0),(-1,1),(1,-1),(1,1),(0,2),(2,0),(-1,2),(2,-1),(1,2),(2,1),(2,2))
-PR=48
-ORDERS=(("x","y","z"),("y","z","x"),("z","x","y"))
-JS=(2,1,-1,0)
+RA=512
+RQ=1024-RA
 
 def nt(a,b): return lax.dot_general(a,b,(((1,),(1,)),((),())),preferred_element_type=F32)
 def nn(a,b): return jnp.dot(a,b,preferred_element_type=F32)
 
-def expert_kernel(hid, gra, ext, wg_hbm, wu_hbm, wd_hbm, D, gq, wg, wu, wd, xh, xg, ga, ex, rs, rr, onehot, prob, sprob, qb,
-                  gate, up, back, gg, ug, spt, own_sem, wsem, qsem, dsem, send_sem, recv_sem):
+def expert_kernel(hid, gra, ext, wg_hbm, wu_hbm, wd_hbm, ws_out, oh_out, rr_out, gq, wg, wu, wd, xh, xg, ga, ex, rs, rr, onehot, prob, sprob, qb,
+                  gate, up, back, gg, ug, spt, own_sem, wsem, qsem, send_sem, recv_sem):
     dp = lax.axis_index("dp"); y = lax.axis_index("tensor")
     x = dp // 8; z = (dp // 2) % 4; c = dp % 2
     here = {"x": x, "y": y, "z": z}
@@ -257,7 +255,12 @@
         def _(kk):
             cols = pl.ds(pl.multiple_of(kk * 512, 512), 512)
             xh[e, rows, cols] = (nt(gg[...], wg[e, cols, :]) + nt(ug[...], wu[e, cols, :])).astype(BF)
-
+        out_copies.append(pltpu.make_async_copy(xh.at[e, rows], ws_out.at[e, rows], wsem.at[3 + h * 2 + e]))
+        out_copies[-1].start()
+
+    out_copies = []
+    oh_copy = pltpu.make_async_copy(onehot, oh_out, own_sem.at[0])
+    oh_copy.start()
     S = {}
     forward("a", 2, -1)
     pack_own(0); S[0] = Slots(0)
@@ -297,7 +300,6 @@
     pack_rest((4, 5, 6, 7))
     for g in range(4, 8): S[g].finish()
     for e in range(2): hidden_units(1, e)
-    for s in pending: s.wait_send()
 
     for g in range(8):
         for e in range(2):
@@ -306,48 +308,37 @@
             for i in range(4):
                 spt[e, g * 4 + i:g * 4 + i + 1, :] = row[:, i * 128:(i + 1) * 128]
     n0 = (dp * 2).astype(F32)
-    first = lax.broadcasted_iota(jnp.int32, (32, 16, 128), 1) == 0
-    for k in range(8):
+    line = lax.broadcasted_iota(jnp.int32, (32, 16, 128), 1)
+    def routed(k):
         r = rs[0, :, k * 128:(k + 1) * 128]
-        v = jnp.where(r == n0, spt[0], 0.0) + jnp.where(r == n0 + 1.0, spt[1], 0.0)
-        rr[:, :, k * 128:(k + 1) * 128] = jnp.where(first, v[:, None, :], 0.0).astype(BF)
-
-    def d_copies(g, t):
-        s = t % 2
-        return [pltpu.make_async_copy(xg.at[s, pl.ds(i * OROWS, OROWS), pl.ds(0, 1024)],
-                    D.at[t, place[2 * g + i // 2][0], place[2 * g + i // 2][1], i % 2], dsem.at[s, i]) for i in range(4)]
-    for g in range(8):
-        oht = onehot[g].astype(F32).T.astype(BF)
-        for t in range(4):
-            n = g * 4 + t
-            if n >= 2:
-                for w in d_copies((n - 2) // 4, (n - 2) % 4): w.wait()
-            v = jnp.concatenate([xh[e, g * 80:(g + 1) * 80, t * 1024:(t + 1) * 1024] for e in range(2)], axis=0)
-            out = nn(oht, v).astype(BF)
-            for i in range(4):
-                xg[t % 2, i * OROWS:i * OROWS + 128, 0:1024] = out[i * 128:(i + 1) * 128]
-                xg[t % 2, i * OROWS + 128:(i + 1) * OROWS, 0:1024] = rr[g * 4 + i]
-            for w in d_copies(g, t): w.start()
-    for n in (30, 31):
-        for w in d_copies(n // 4, n % 4): w.wait()
+        return (jnp.where(r == n0, spt[0], 0.0) + jnp.where(r == n0 + 1.0, spt[1], 0.0))[:, None, :]
+    for k in range(4):
+        rr[:, :, k * 128:(k + 1) * 128] = (jnp.where(line == 0, routed(k), 0.0) + jnp.where(line == 1, routed(k + 4), 0.0)).astype(BF)
+    rr_copy = pltpu.make_async_copy(rr, rr_out, own_sem.at[1])
+    rr_copy.start()
+    oh_copy.wait()
+    for w in out_copies: w.wait()
+    rr_copy.wait()
+    for s in pending: s.wait_send()
 
 def experts(hid, gra, ext, wg, wu, wd):
     V=pltpu.VMEM
     A=pl.BlockSpec(memory_space=pl.ANY)
     N=4 + 3 + 7 + 4 + 2 * (40 + 32) + 64
     return pl.pallas_call(expert_kernel,
-        out_shape=(jax.ShapeDtypeStruct((4,4,4,2,OROWS,1024),BF), jax.ShapeDtypeStruct((4,4,2,4,128,CQ),BF)),
-        in_specs=[A]*6, out_specs=(A,A),
+        out_shape=(jax.ShapeDtypeStruct((2,640,4096),BF), jax.ShapeDtypeStruct((8,160,512),BF), jax.ShapeDtypeStruct((32,16,512),BF), jax.ShapeDtypeStruct((4,4,2,4,128,CQ),BF)),
+        in_specs=[A]*6, out_specs=(A,)*4,
         scratch_shapes=[V((2,4096,384),BF),V((2,4096,384),BF),V((2,384,4096),BF),
-            V((2,640,4096),BF),V((2,640,4096),BF),V((4,4,2,128,CA),BF),V((4,4,2,16,1024),BF),V((3,32,1024),F32),V((32,16,1024),BF),
+            V((2,640,4096),BF),V((2,640,4096),BF),V((4,4,2,128,CA),BF),V((4,4,2,16,1024),BF),V((3,32,1024),F32),V((32,16,512),BF),
             V((8,160,512),BF),V((2,640,128),F32),V((2,640,128),F32),V((4,2,2,128,CQ),BF),
             V((320,384),F32),V((320,384),F32),V((320,384),F32),V((320,384),BF),V((320,384),BF),V((2,32,128),F32),
-            pltpu.SemaphoreType.DMA((5,)),pltpu.SemaphoreType.DMA((3,)),pltpu.SemaphoreType.DMA((4,2)),pltpu.SemaphoreType.DMA((2,4)),
+            pltpu.SemaphoreType.DMA((5,)),pltpu.SemaphoreType.DMA((7,)),pltpu.SemaphoreType.DMA((4,2)),
             pltpu.SemaphoreType.DMA((N,)),pltpu.SemaphoreType.DMA((N,))],
         compiler_params=pltpu.CompilerParams(collective_id=0, has_side_effects=True, vmem_limit_bytes=63*1024*1024),
-    )(hid, gra, ext, wg, wu, wd)[0]
-
-def return_kernel(D, pick, grad, router, sib, own, r1, r2, r3, m2, m3, fin, inc, own_sem, send_sem, recv_sem):
+    )(hid, gra, ext, wg, wu, wd)[:3]
+
+def return_kernel(ws_hbm, oh_hbm, rr_hbm, pick, grad, router, ws, onehot, rr, y1, y2, red, pq, sq, lq, pa, sa, la, ly, lr, fin, inc,
+                  in_sem, g_sem, send_sem, recv_sem):
     dp = lax.axis_index("dp"); y = lax.axis_index("tensor")
     x = dp // 8; z = (dp // 2) % 4; c = dp % 2
     here = {"x": x, "y": y, "z": z}
@@ -361,8 +352,14 @@
     for bit in range(3):
         low = (dp // (1 << bit)) % 2
         mates.append({"dp": dp + (1 - 2 * low) * (1 << bit), "tensor": y})
+    def g_copy(g):
+        rows = pl.ds(g * 80, 80)
+        return pltpu.make_async_copy(ws_hbm.at[:, rows], ws.at[:, rows], g_sem.at[g])
+    small = [pltpu.make_async_copy(oh_hbm, onehot, in_sem.at[0]), pltpu.make_async_copy(rr_hbm, rr, in_sem.at[1])]
+    for s in small: s.start()
+    for g in reversed(range(8)): g_copy(g).start()
     barrier = pltpu.get_barrier_semaphore()
-    partners = [device(a, s) for a in "xyz" for s in (1, -1)] + mates
+    partners = [device(a, s) for a in "xyz" for s in (1, -1)] + [device("y", 2)] + mates
     for p in partners:
         pl.semaphore_signal(barrier, inc=1, device_id=p, device_id_type=MESH)
     pl.semaphore_wait(barrier, len(partners))
@@ -376,98 +373,158 @@
         copy.start()
         pending.append(copy)
         return copy
-    def block(p, j, k, core):
-        A, B, C = ORDERS[p]
-        at = {A: None, B: (here[B] + j + 4) % 4, C: (here[C] + k + 4) % 4}
-        idx = tuple(pl.ds(0, 4) if at[a] is None else at[a] for a in "yxz")
-        return D.at[idx + (core, pl.ds(p * PR, PR))]
-    order = [(p, j, k) for j in JS for k in JS for p in range(3)]
-    sibs = {}
-    for p, j, k in order:
-        sibs[p, j, k] = send(block(p, j, k, 1 - c), sib.at[p, JS.index(j), JS.index(k)], device("c", 0))
-    NB = 6
-    def own_copy(n):
-        p, j, k = order[n]
-        return pltpu.make_async_copy(block(p, j, k, c), own.at[n % NB], own_sem.at[n % NB])
-    for n in range(NB): own_copy(n).start()
     def add(dst, *terms):
-        @pl.loop(0, dst.shape[0])
-        def _(i):
-            total = terms[0][i].astype(F32)
-            for t in terms[1:]: total = total + t[i].astype(F32)
-            dst[i] = total.astype(BF)
-    done = [0]
-    def merge(p, j, k):
-        n = done[0]; done[0] += 1
-        assert order[n] == (p, j, k)
-        own_copy(n).wait()
-        sibs[p, j, k].wait_recv()
-        m = sib.at[p, JS.index(j), JS.index(k)]
-        add(m, m, own.at[n % NB])
-        if n + NB < len(order): own_copy(n + NB).start()
-        return m
+        if len(dst.shape) == 3:
+            @pl.loop(0, dst.shape[0])
+            def _(i):
+                total = terms[0][i].astype(F32)
+                for t in terms[1:]: total = total + t[i].astype(F32)
+                dst[i] = total.astype(BF)
+        else:
+            total = terms[0][...].astype(F32)
+            for t in terms[1:]: total = total + t[...].astype(F32)
+            dst[...] = total.astype(BF)
     class Ring:
-        def __init__(self, axis, land):
+        def __init__(self, axis, land, far_up, far_down):
             self.axis, self.land = axis, land
-        def start(self, far):
-            a = self.axis
-            self.up1 = send(far.at[0:2], self.land.at[0:2], device(a, 1))
-            self.down1 = send(far.at[2:4], self.land.at[2:4], device(a, -1))
-        def middle(self, after, before):
-            a = self.axis
+            self.up1 = send(far_up, land[0], device(axis, 1))
+            self.down1 = send(far_down, land[1], device(axis, -1))
+        def middle(self, after, after_up, before, before_down):
             self.up1.wait_recv()
-            lo = after.at[0:2]
-            add(lo, lo, self.land.at[0:2])
-            self.up2 = send(after, self.land.at[4:8], device(a, 1))
+            add(after_up, after_up, self.land[0])
+            self.up2 = send(after, self.land[2], device(self.axis, 1))
             self.down1.wait_recv()
-            hi = before.at[2:4]
-            add(hi, hi, self.land.at[2:4])
-            self.down2 = send(before, self.land.at[8:12], device(a, -1))
-        def finish(self, near, out):
+            add(before_down, before_down, self.land[1])
+            self.down2 = send(before, self.land[3], device(self.axis, -1))
+        def finish(self, near):
             self.up2.wait_recv(); self.down2.wait_recv()
-            add(out, near, self.land.at[4:8], self.land.at[8:12])
-    rings = {}
-    M = {}
-    def first(j):
-        for k in JS:
-            for p in range(3):
-                M[p, j, k] = merge(p, j, k)
-                if k == 2:
-                    r = rings[p, j] = Ring(ORDERS[p][2], r1.at[p, JS.index(j)])
-                    r.start(M[p, j, 2])
-    def second(j):
-        for p in range(3): rings[p, j].middle(M[p, j, 1], M[p, j, -1])
-    def third(j):
-        for p in range(3): rings[p, j].finish(M[p, j, 0], m2.at[p, JS.index(j)])
-    late = {}
-    first(2); first(1); second(2); first(-1); second(1); third(2)
-    for p in range(3):
-        late[p] = Ring(ORDERS[p][1], r2.at[p]); late[p].start(m2.at[p, 0])
-    first(0); second(-1); third(1); second(0); third(-1)
-    for p in range(3): late[p].middle(m2.at[p, 1], m2.at[p, 2])
-    third(0)
-    for p in range(3): late[p].finish(m2.at[p, 3], m3.at[p])
-    last = {}
-    cut = [pl.ds(0, 512), pl.ds(512, 512)]
-    for p in range(3):
-        A = ORDERS[p][0]
-        far = m3.at[p, (here[A] + 2) % 4]
-        last[p] = [send(far.at[:, cut[0]], r3.at[p, 0, :, cut[0]], device(A, 1)),
-                   send(far.at[:, cut[1]], r3.at[p, 0, :, cut[1]], device(A, -1))]
-    for p in range(3):
-        A = ORDERS[p][0]
-        for s in (0, 1):
-            last[p][s].wait_recv()
-            m = m3.at[p, (here[A] + (1, 3)[s]) % 4]
-            m[:, cut[s]] = (m[:, cut[s]].astype(F32) + r3[p, 0, :, cut[s]].astype(F32)).astype(BF)
-            last[p].append(send(m, r3.at[p, 1 + s], device(A, (1, -1)[s])))
-    for p in range(3):
-        A = ORDERS[p][0]
-        last[p][2].wait_recv(); last[p][3].wait_recv()
-        total = m3[p, here[A]].astype(F32) + r3[p, 1].astype(F32) + r3[p, 2].astype(F32)
-        fin[p * PR:(p + 1) * PR, :] = total.astype(BF)
+            add(near, near, self.land[2], self.land[3])
+
+    def slot(g, k, es=pl.ds(0, 2)):
+        at = pl.multiple_of(((y + k + 4) % 4) * 1024, 1024)
+        return ws.at[es, pl.ds(g * 80, 80), pl.ds(at, RA)]
+    Y = {}
+    def y_start(g):
+        Y[g] = Ring("y", (y1.at[g, pl.ds(0, 1)], y1.at[g, pl.ds(1, 1)], y2.at[g, 0], y2.at[g, 1]),
+                    slot(g, 2, pl.ds(0, 1)), slot(g, 2, pl.ds(1, 1)))
+    def y_middle(g):
+        Y[g].middle(slot(g, 1), slot(g, 1, pl.ds(0, 1)), slot(g, -1), slot(g, -1, pl.ds(1, 1)))
+    def y_finish(g):
+        Y[g].finish(slot(g, 0))
+    def spread(g):
+        return onehot[g].astype(F32).T.astype(BF)
+    sib = {}
+    def combine_rest(g):
+        oht = spread(g)
+        for t in range(4):
+            v = jnp.concatenate([ws[e, g * 80:(g + 1) * 80, t * 1024 + RA:(t + 1) * 1024] for e in range(2)], axis=0)
+            out = nn(oht, v).astype(BF)
+            for i in range(4):
+                pq[i % 2, 2 * g + i // 2, t] = out[i * 128:(i + 1) * 128]
+        for n in (2 * g + 1, 2 * g):
+            sib["q", n] = send(pq.at[1 - c, n], sq.at[n], device("c", 0))
+    def combine_own(g):
+        oht = spread(g)
+        at = pl.ds(pl.multiple_of(y * 1024, 1024), RA)
+        v = jnp.concatenate([ws[e, g * 80:(g + 1) * 80, at] for e in range(2)], axis=0)
+        out = nn(oht, v).astype(BF)
+        for i in range(4):
+            pa[i % 2, 2 * g + i // 2, 16:144] = out[i * 128:(i + 1) * 128]
+            pa[i % 2, 2 * g + i // 2, 0:16] = rr[g * 4 + i]
+        for n in (2 * g + 1, 2 * g):
+            sib["a", n] = send(pa.at[1 - c, n], sa.at[n], device("c", 0))
+    def merge(q, n):
+        sib[q, n].wait_recv()
+        if q == "q":
+            add(pq.at[c, n], pq.at[c, n], sq.at[n])
+        else:
+            add(pa.at[c, n], pa.at[c, n], sa.at[n])
+    def block(q, f, n, part="all"):
+        if q == "q":
+            ts = {"all": pl.ds(0, 4), "up": pl.ds(0, 2), "down": pl.ds(2, 2)}[part]
+            return pq.at[c, n, ts, pl.ds(64 * f, 64)]
+        first, count = {"all": ((0, 80), (80, 64)), "up": ((0, 48), (80, 32)), "down": ((48, 32), (112, 32))}[part][f]
+        return pa.at[c, n, pl.ds(first, count)]
+    def land(q, f, r):
+        if q == "q":
+            v = lq.at[f, r]
+            return v.at[pl.ds(0, 2)], v.at[pl.ds(2, 2)], v.at[pl.ds(4, 4)], v.at[pl.ds(8, 4)]
+        up, down = ((48, 32), (32, 32))[f]
+        v = la.at[f, r]
+        return v.at[pl.ds(0, up)], v.at[pl.ds(48, down)], v.at[pl.ds(80, up + down)], v.at[pl.ds(160, up + down)]
+    R = {}
+    def chip(f, s, k):
+        return CHIPS.index((s, k) if f == 0 else (k, s))
+    def start_one(q, s):
+        for f in (0, 1):
+            n = chip(f, s, 2)
+            R[q, f, s] = Ring("zx"[f], land(q, f, STEPS.index(s)), block(q, f, n, "up"), block(q, f, n, "down"))
+    def middle_one(q, s):
+        for f in (0, 1):
+            a, b = chip(f, s, 1), chip(f, s, -1)
+            R[q, f, s].middle(block(q, f, a), block(q, f, a, "up"), block(q, f, b), block(q, f, b, "down"))
+    def finish_one(q, s):
+        for f in (0, 1): R[q, f, s].finish(block(q, f, chip(f, s, 0)))
+    def start_two(q):
+        for f in (0, 1):
+            n = chip(f, 2, 0)
+            R[q, f, "two"] = Ring("xz"[f], land(q, f, 4), block(q, f, n, "up"), block(q, f, n, "down"))
+    def middle_two(q):
+        for f in (0, 1):
+            a, b = chip(f, 1, 0), chip(f, -1, 0)
+            R[q, f, "two"].middle(block(q, f, a), block(q, f, a, "up"), block(q, f, b), block(q, f, b, "down"))
+    def finish_two(q):
+        for f in (0, 1): R[q, f, "two"].finish(block(q, f, 0))
+
+    for s in small: s.wait()
+    for g in reversed(range(8)):
+        g_copy(g).wait()
+        y_start(g)
+        combine_rest(g)
+    for n in range(15, 8, -1): merge("q", n)
+    for s in (2, 1, -1, 0): start_one("q", s)
+    y_middle(7); y_middle(6)
+    for n in range(8, 3, -1): merge("q", n)
+    middle_one("q", 2)
+    y_middle(5); y_middle(4)
+    middle_one("q", 1)
+    for n in range(3, -1, -1): merge("q", n)
+    y_middle(3); y_middle(2)
+    middle_one("q", -1)
+    middle_one("q", 0)
+    y_middle(1); y_middle(0)
+    finish_one("q", 2)
+    start_two("q")
+    for g in (7, 6, 5, 4):
+        y_finish(g); combine_own(g)
+    finish_one("q", 1); finish_one("q", -1)
+    middle_two("q")
+    for g in (3, 2, 1, 0):
+        y_finish(g); combine_own(g)
+    for n in range(15, 8, -1): merge("a", n)
+    for s in (2, 1, -1, 0): start_one("a", s)
+    finish_one("q", 0)
+    for n in range(8, -1, -1): merge("a", n)
+    for s in (2, 1, -1, 0): middle_one("a", s)
+    finish_two("q")
+    def rest(k, part=pl.ds(0, 128)):
+        return pq.at[c, 0, (y + k + 4) % 4, part]
+    lo, hi = pl.ds(0, 64), pl.ds(64, 64)
+    last = Ring("y", (ly.at[pl.ds(0, 64)], ly.at[pl.ds(64, 64)], ly.at[pl.ds(128, 128)], ly.at[pl.ds(256, 128)]), rest(2, lo), rest(2, hi))
+    finish_one("a", 2)
+    start_two("a")
+    finish_one("a", 1); finish_one("a", -1)
+    middle_two("a")
+    last.middle(rest(1), rest(1, lo), rest(-1), rest(-1, hi))
+    finish_one("a", 0)
+    finish_two("a")
+    odds = [send(pa.at[c, 0, pl.ds(0, 16)], lr.at[i], device("y", s)) for i, s in enumerate((1, 2, -1))]
+    fin[:, 0:RA] = pa[c, 0, 16:144]
+    last.finish(rest(0))
+    fin[:, RA:1024] = pq[c, 0, y]
     swaps = [send(fin.at[64:128], inc.at[b], mates[b]) for b in range(3)]
-    router[...] = fin[128:144, :]
+    for o in odds: o.wait_recv()
+    router[...] = (pa[c, 0, 0:16].astype(F32) + lr[0].astype(F32) + lr[1].astype(F32) + lr[2].astype(F32)).astype(BF)
     grad[0:64, :] = fin[0:64, :]
     for s in swaps: s.wait_recv()
     row = lax.broadcasted_iota(jnp.int32, (64, 1024), 0)
@@ -478,18 +535,22 @@
     grad[64:128, :] = kept.astype(BF)
     for s in pending: s.wait_send()
 
-def returned(D, pick):
+def returned(ws, oh, rr, pick):
     V=pltpu.VMEM
-    N=48 + 3 * 4 * 4 + 3 * 4 + 3 * 4 + 3
+    A=pl.BlockSpec(memory_space=pl.ANY)
+    N=16 + 16 + 40 + 40 + 32 + 4 + 3 + 3
     return pl.pallas_call(return_kernel,
-        out_shape=(jax.ShapeDtypeStruct((128,1024),BF),jax.ShapeDtypeStruct((16,1024),BF)),
-        in_specs=[pl.BlockSpec(memory_space=pl.ANY),pl.BlockSpec(memory_space=pltpu.SMEM)],
+        out_shape=(jax.ShapeDtypeStruct((128,1024),BF),jax.ShapeDtypeStruct((16,RA),BF)),
+        in_specs=[A,A,A,pl.BlockSpec(memory_space=pltpu.SMEM)],
         out_specs=(pl.BlockSpec(memory_space=V),pl.BlockSpec(memory_space=V)),
-        scratch_shapes=[V((3,4,4,4,PR,1024),BF),V((6,4,PR,1024),BF),V((3,4,12,PR,1024),BF),V((3,12,PR,1024),BF),
-            V((3,3,PR,1024),BF),V((3,4,4,PR,1024),BF),V((3,4,PR,1024),BF),V((OROWS,1024),BF),V((3,64,1024),BF),
-            pltpu.SemaphoreType.DMA((6,)),pltpu.SemaphoreType.DMA((N,)),pltpu.SemaphoreType.DMA((N,))],
-        compiler_params=pltpu.CompilerParams(collective_id=1, has_side_effects=True, vmem_limit_bytes=62*1024*1024),
-    )(D, pick)
+        scratch_shapes=[V((2,640,4096),BF),V((8,160,512),BF),V((32,16,RA),BF),
+            V((8,2,80,RA),BF),V((8,2,2,80,RA),BF),V((8,128),F32),
+            V((2,16,4,128,RQ),BF),V((16,4,128,RQ),BF),V((2,5,12,64,RQ),BF),
+            V((2,16,144,RA),BF),V((16,144,RA),BF),V((2,5,240,RA),BF),
+            V((384,RQ),BF),V((3,16,RA),BF),V((128,1024),BF),V((3,64,1024),BF),
+            pltpu.SemaphoreType.DMA((2,)),pltpu.SemaphoreType.DMA((8,)),pltpu.SemaphoreType.DMA((N,)),pltpu.SemaphoreType.DMA((N,))],
+        compiler_params=pltpu.CompilerParams(collective_id=1, has_side_effects=True, vmem_limit_bytes=63*1024*1024),
+    )(ws, oh, rr, pick)
 
 def local(hidden, grad_out, routes, route_probs, w_gate, w_up, w_down, partner, swap_count):
     flat = route_probs.T.reshape(1, 1024)
@@ -497,12 +558,12 @@
     low = (flat - high.astype(F32)).astype(BF)
     number = routes.T.reshape(1, 1024).astype(BF)
     ext = jnp.concatenate([number, high, low, jnp.zeros((13, 1024), BF)], axis=0)
-    partial = experts(hidden, grad_out, ext, w_gate, w_up, w_down)
+    ws, oh, rr = experts(hidden, grad_out, ext, w_gate, w_up, w_down)
     rank = lax.axis_index("dp")
     apart = jnp.bitwise_xor(partner[rank], rank)
     pick = jnp.stack([apart // 2, swap_count[rank]]).astype(jnp.int32)
-    grad, router = returned(partial, pick)
-    return grad, router[0].reshape(8, 128).T
+    grad, router = returned(ws, oh, rr, pick)
+    return grad, router[:2].reshape(8, 128).T
 
 
 def solution(mesh):

time: 296 us -> 265 us (0.90)
  Pallas kernels: 286 us -> 256 us
    pallas_call x1, Pallas kernels: 193 us -> 170 us  [experts(): pl.pallas_call(expert_kernel, out_shape=(jax.ShapeDtypeStruct((2, 640, 40...]
    pallas_call x1, Pallas kernels: 92.8 us -> 85.1 us  [returned(): pl.pallas_call(return_kernel, out_shape=(jax.ShapeDtypeStruct((128, 1024)...]
where the time goes in v2:
time: 265 us; the launch traced here: 264 us
  Pallas kernels  256 us (97%)
  local copies, waits for them, and re-layouts  4.22 us (2%)
  other arithmetic  3.32 us (1%)
    pallas_call x1, Pallas kernels, experts(): pl.pallas_call(expert_kernel, out_shape=(jax.ShapeDtypeStruct((2, 640, 40...  170 us
    pallas_call x1, Pallas kernels, returned(): pl.pallas_call(return_kernel, out_shape=(jax.ShapeDtypeStruct((128, 1024)...  85.1 us

profile of v2, /device:TPU:0, one launch (start us, length us, event | category | flops | bytes accessed | tf_op | source)
XLA Modules:
  0.0 264.4 jit_solution(9602216604925587471)
XLA Ops:
  0.6 0.7 reduce-precision_convert_fusion
  1.3 0.7 convert_bitcast_fusion
  2.0 0.1 pad.5.clone
  2.1 0.7 maximum_maximum_fusion.ext
  2.8 0.0 copy-start
  2.8 0.0 copy-start.1
  2.8 170.4 %shard_map.104 = (bf16[2,640,4096]{2,1,0:T(8,128)(2,1)}, bf16[8,160,512]{2,1,0:T(8,128)(2,1)}, bf16[32,16,512]{2,1,0:T(8,128)(2,1)}, bf16[4,4,2,4,128,896]{5,4,3,2,1,0:T(8,128)(2,1)}) custom-call(bf16[128,1024]{1,0:T(8,128)(2,1)} %hid.1, bf16[128,1024]{1,0:T(8,128)(2,1)} %gra.1, bf16[16,1024]{1,0:T(8,128)(2,1)} %maximum_maximum_fusion.ext, ...), custom_call_target="tpu_custom_call" | custom-call | tf_op jit(solution)/shard_map/pallas_call | solution.py:328
  173.3 0.0 copy-done
  173.3 0.6 dynamic_slice.7
  173.9 0.0 copy-done.1
  173.9 0.6 dynamic_slice.6
  175.1 1.2 pad_add_fusion.pick
  176.4 85.1 %shard_map.105 = (bf16[128,1024]{1,0:T(8,128)(2,1)}, bf16[16,512]{1,0:T(8,128)(2,1)}) custom-call(bf16[2,640,4096]{2,1,0:T(8,128)(2,1)} %get-tuple-element.7.ws_hbm, bf16[8,160,512]{2,1,0:T(8,128)(2,1)} %get-tuple-element.8.oh_hbm, bf16[32,16,512]{2,1,0:T(8,128)(2,1)} %get-tuple-element.9.rr_hbm, s32[2]{0:T(128)} %pad_add_fusion.pick), custom_call_target="tpu_custom_call" | custom-call | tf_op jit(solution)/shard_map/pallas_call | solution.py:542
  261.5 0.7 slice.3
  262.2 0.6 reshape.65
  262.8 1.7 copy.15
  (2 shorter events, 0.0 us)
Async XLA Ops:
  2.8 170.5 %copy-start = (s32[32]{0:T(128)S(1)}, s32[32]{0:T(128)}, u32[]{:S(2)}) copy-start(s32[32]{0:T(128)} %param.17) | copy-start | bytes 388
  2.8 171.1 %copy-start.1 = (s32[32]{0:T(128)S(1)}, s32[32]{0:T(128)}, u32[]{:S(2)}) copy-start(s32[32]{0:T(128)} %param.16) | copy-start | bytes 388

commit v3 on v2

--- a/solution.py
+++ b/solution.py
@@ -20,8 +20,8 @@
 def nt(a,b): return lax.dot_general(a,b,(((1,),(1,)),((),())),preferred_element_type=F32)
 def nn(a,b): return jnp.dot(a,b,preferred_element_type=F32)
 
-def expert_kernel(hid, gra, ext, wg_hbm, wu_hbm, wd_hbm, ws_out, oh_out, rr_out, gq, wg, wu, wd, xh, xg, ga, ex, rs, rr, onehot, prob, sprob, qb,
-                  gate, up, back, gg, ug, spt, own_sem, wsem, qsem, send_sem, recv_sem):
+def expert_kernel(hid, gra, routes_ref, probs_ref, wg_hbm, wu_hbm, wd_hbm, ws_out, oh_out, rr_out, gq, wgu, wd, xh, xg, ga, qo, ex, rs, rr, onehot, prob, sprob, qb,
+                  gu, back, ggu, spt, own_sem, wsem, qsem, send_sem, recv_sem):
     dp = lax.axis_index("dp"); y = lax.axis_index("tensor")
     x = dp // 8; z = (dp // 2) % 4; c = dp % 2
     here = {"x": x, "y": y, "z": z}
@@ -32,9 +32,18 @@
         at[axis] = (at[axis] + step + 4) % 4
         return {"dp": at["x"] * 8 + at["z"] * 2 + c, "tensor": at["y"]}
     barrier = pltpu.get_barrier_semaphore()
-    partners = [device(a, s) for a in "xyz" for s in (1, -1)] + [device("c", 0)]
+    partners = [device(a, s) for a in "xyz" for s in (1, -1)] + [device("x", 2), device("z", 2), device("c", 0)]
     for p in partners:
         pl.semaphore_signal(barrier, inc=1, device_id=p, device_id_type=MESH)
+    probs = probs_ref[...]
+    high = probs.astype(BF).astype(F32)
+    ex[x, z, c] = jnp.concatenate([routes_ref[...].astype(F32), high, probs - high, jnp.zeros((8, 128), F32)], axis=0).astype(BF)
+    ga[x, z, c, :, 0:HA] = hid[:, 0:HA]
+    ga[x, z, c, :, HA:CA] = gra[:, 0:GA]
+    qo[:, 0:1024 - HA] = hid[:, HA:1024]
+    qo[:, 1024 - HA:CQ] = gra[:, GA:1024]
+    keep = pltpu.make_async_copy(qo, gq.at[x, z, c, y], own_sem.at[0])
+    keep.start()
     pl.semaphore_wait(barrier, len(partners))
 
     number = [0]
@@ -46,19 +55,8 @@
         copy.start()
         pending.append(copy)
         return copy
-    mine = [pltpu.make_async_copy(a, b, own_sem.at[i]) for i, (a, b) in enumerate((
-        (ext, ex.at[x, z, c]),
-        (hid.at[:, pl.ds(0, HA)], ga.at[x, z, c, :, pl.ds(0, HA)]),
-        (gra.at[:, pl.ds(0, GA)], ga.at[x, z, c, :, pl.ds(HA, GA)]),
-        (hid.at[:, pl.ds(HA, 1024 - HA)], gq.at[x, z, c, y, :, pl.ds(0, 1024 - HA)]),
-        (gra.at[:, pl.ds(GA, 1024 - GA)], gq.at[x, z, c, y, :, pl.ds(1024 - HA, 1024 - GA)])))]
-    for m in mine: m.start()
-    for m in mine: m.wait()
-
     def view(fam, at, part="all"):
         xx = pl.ds(0, 4) if at["x"] is None else at["x"]
-        if fam == "E":
-            return ex.at[xx, at["z"], c]
         if fam in ("alo", "ahi"):
             first = 0 if fam == "alo" else 64
             first, count = {"all": (first, 64), "up": (first, 32), "down": (first + 32, 32)}[part]
@@ -77,11 +75,11 @@
         q = dict(at); q[axis] = (here[axis] + step + 4) % 4
         return q
     class Ring:
-        def __init__(self, fam, axis, at, off):
+        def __init__(self, fam, axis, at, off, src=None):
             self.fam, self.axis, self.at, self.off = fam, axis, at, off
             v = view(fam, at)
-            self.up = send(v, v, device(axis, 1))
-            self.down = send(v, v, device(axis, -1))
+            self.up = send(v if src is None else src, v, device(axis, 1))
+            self.down = send(v if src is None else src, v, device(axis, -1))
         def key(self, step):
             if self.off is None: return None
             o = dict(self.off); o[self.axis] = step
@@ -94,14 +92,12 @@
             self.up2 = send(v, v, device(a, 1))
             to_sibling(f, before, self.key(-1))
             self.down.wait_recv()
-            self.down2 = None
-            if f != "E":
-                v = view(f, after, "down")
-                self.down2 = send(v, v, device(a, -1))
+            v = view(f, after, "down")
+            self.down2 = send(v, v, device(a, -1))
             to_sibling(f, after, self.key(1))
         def finish(self):
             self.up2.wait_recv()
-            if self.down2 is not None: self.down2.wait_recv()
+            self.down2.wait_recv()
             to_sibling(self.fam, moved(self.at, self.axis, 2), self.key(2))
     def sets(q):
         return ((q + "lo", "x", "z"), (q + "hi", "z", "x"))
@@ -121,43 +117,32 @@
     def finish(q, *which):
         for f, a, b in sets(q): R[(f,) + which].finish()
 
-    e1 = Ring("E", "x", here, zero)
-    qy = Ring("Q", "y", here, None)
+    def table_sends(v, to):
+        return [send(v, v, d) for d in to]
+    e = table_sends(ex.at[x, z, c], [device("c", 0)])
+    qy = Ring("Q", "y", here, None, qo)
     stage_one("a")
-    to_sibling("E", here, (0, 0))
-    weights = [pltpu.make_async_copy(a, b, wsem.at[i]) for i,(a,b) in enumerate(((wg_hbm,wg),(wu_hbm,wu),(wd_hbm,wd)))]
-    e1.forward()
+    weights = [pltpu.make_async_copy(a, b, wsem.at[i]) for i,(a,b) in enumerate(((wg_hbm, wgu.at[:, :, pl.ds(0, 384)]), (wu_hbm, wgu.at[:, :, pl.ds(384, 384)]), (wd_hbm, wd)))]
+    for w in e: w.wait_recv()
+    e = table_sends(ex.at[x, z], [device("x", s) for s in (1, 2, -1)])
     forward("a", 1)
     stage_two("a", (-1, 1))
-    e1.finish()
-    def e_sib(step):
-        at = moved(here, "z", step); at["x"] = None
-        v = view("E", at)
-        sibs["E", "col", step] = send(v, v, device("c", 0))
-    col = dict(here); col["x"] = None
-    e2 = Ring("E", "z", col, None)
+    for w in e: w.wait_recv()
+    e = table_sends(ex.at[:, z], [device("z", s) for s in (1, 2, -1)])
+    qy.forward()
     finish("a", 1)
     stage_two("a", (2,))
-    qy.forward()
-    e2.forward()
-    e_sib(-1); e_sib(1)
-    forward("a", 2, 0)
-    qy.finish()
-    stage_one("q")
-    e2.finish()
-    e_sib(2)
+    for w in e: w.wait_recv()
     for w in weights: w.start()
-    for k in ((0, 0), (-1, 0), (1, 0), (2, 0)): sibs[("E",) + k].wait_recv()
-    for s in (-1, 1, 2): sibs["E", "col", s].wait_recv()
 
     place = [((x + dx + 4) % 4, (z + dz + 4) % 4) for dx, dz in CHIPS]
     for n, (px, pz) in enumerate(place):
         for s in range(2):
             block = ex[px, pz, s].astype(F32)
-            for q in range(3):
+            for q in range(24):
                 rs[q, 2 * n + s:2 * n + s + 1, :] = block[q:q + 1]
-    routes = [rs[0, :, k * 128:(k + 1) * 128] for k in range(8)]
-    probs = [rs[1, :, k * 128:(k + 1) * 128] + rs[2, :, k * 128:(k + 1) * 128] for k in range(8)]
+    routes = [rs[k] for k in range(8)]
+    probs = [rs[8 + k] + rs[16 + k] for k in range(8)]
     tri = (lax.broadcasted_iota(jnp.int32, (128, 128), 0) < lax.broadcasted_iota(jnp.int32, (128, 128), 1)).astype(F32).astype(BF)
     for e in range(2):
         name = (dp * 2 + e).astype(F32)
@@ -176,6 +161,10 @@
             onehot[g, e * 80:(e + 1) * 80, :] = oh.astype(BF)
             prob[e, g * 80:(g + 1) * 80, :] = jnp.broadcast_to(jnp.sum(oh * w4, axis=1, keepdims=True), (80, 128))
 
+    forward("a", 2, 0)
+    qy.finish()
+    keep.wait()
+    stage_one("q")
     waited = set()
     def need(q, g):
         for key in CHIPS[2 * g:2 * g + 2]:
@@ -230,36 +219,47 @@
                     xg[e, rows, yy * 1024 + GA:(yy + 1) * 1024] = out[e * 80:(e + 1) * 80, 1024 - HA:]
                 if after is not None:
                     for w in q_copies(after, yy): w.start()
-    def hidden_units(h, e):
-        rows = pl.ds(h * 320, 320)
-        gate[...] = jnp.zeros_like(gate); up[...] = jnp.zeros_like(up); back[...] = jnp.zeros_like(back)
-        @pl.loop(0, 8)
+    spans = ((0, 400), (400, 240))
+    def units_in(h, e):
+        first, count = spans[h]
+        rows = pl.ds(first, count)
+        part = pl.ds(0, count)
+        @pl.loop(0, 4)
         def _(kk):
-            cols = pl.ds(pl.multiple_of(kk * 512, 512), 512)
-            a = xh[e, rows, cols]
-            gate[...] += nn(a, wg[e, cols, :])
-            up[...] += nn(a, wu[e, cols, :])
-            back[...] += nt(xg[e, rows, cols], wd[e, :, cols])
-        @pl.loop(0, 4)
+            cols = pl.ds(pl.multiple_of(kk * 1024, 1024), 1024)
+            both = nn(xh[e, rows, cols], wgu[e, cols, :])
+            last = nt(xg[e, rows, cols], wd[e, :, cols])
+            @pl.when(kk == 0)
+            def _():
+                gu[part] = both
+                back[part] = last
+            @pl.when(kk > 0)
+            def _():
+                gu[part] += both
+                back[part] += last
+    def units_out(h, e):
+        first, count = spans[h]
+        rows = pl.ds(first, count)
+        @pl.loop(0, count // 80)
         def _(r):
             here_rows = pl.ds(pl.multiple_of(r * 80, 16), 80)
-            all_rows = pl.ds(pl.multiple_of(h * 320 + r * 80, 16), 80)
-            gp = gate[here_rows, :]; u = up[here_rows, :]; b = back[here_rows, :]
+            all_rows = pl.ds(pl.multiple_of(first + r * 80, 16), 80)
+            gp = gu[here_rows, 0:384]; u = gu[here_rows, 384:768]; b = back[here_rows, :]
             sig = 1.0 / (1.0 + jnp.exp(-gp))
             act = gp * sig
             sprob[e, all_rows, :] = jnp.broadcast_to(jnp.sum(b * act * u, axis=1, keepdims=True), (80, 128))
             p = prob[e, all_rows, 0:1]
-            gg[here_rows, :] = (b * u * sig * (1.0 + gp * (1.0 - sig)) * p).astype(BF)
-            ug[here_rows, :] = (b * act * p).astype(BF)
-        @pl.loop(0, 8)
+            ggu[here_rows, 0:384] = (b * u * sig * (1.0 + gp * (1.0 - sig)) * p).astype(BF)
+            ggu[here_rows, 384:768] = (b * act * p).astype(BF)
+        @pl.loop(0, 4)
         def _(kk):
-            cols = pl.ds(pl.multiple_of(kk * 512, 512), 512)
-            xh[e, rows, cols] = (nt(gg[...], wg[e, cols, :]) + nt(ug[...], wu[e, cols, :])).astype(BF)
+            cols = pl.ds(pl.multiple_of(kk * 1024, 1024), 1024)
+            xh[e, rows, cols] = nt(ggu[0:count], wgu[e, cols, :]).astype(BF)
         out_copies.append(pltpu.make_async_copy(xh.at[e, rows], ws_out.at[e, rows], wsem.at[3 + h * 2 + e]))
         out_copies[-1].start()
 
     out_copies = []
-    oh_copy = pltpu.make_async_copy(onehot, oh_out, own_sem.at[0])
+    oh_copy = pltpu.make_async_copy(onehot, oh_out, own_sem.at[2])
     oh_copy.start()
     S = {}
     forward("a", 2, -1)
@@ -285,21 +285,26 @@
     S[4].forward(); S[7] = Slots(7)
     forward("q", 2, 1)
     pack_rest((2, 3))
+    finish("q", 2, 0)
+    pack_rest((4,))
     for w in weights: w.wait()
-    for g in range(4): S[g].finish()
-    hidden_units(0, 0)
+    for g in range(5): S[g].finish()
+    units_in(0, 0)
     S[5].forward()
-    finish("q", 2, 0)
+    finish("q", 2, -1)
+    units_out(0, 0)
     forward("q", 2, 2)
-    hidden_units(0, 1)
     S[6].forward()
-    finish("q", 2, -1)
+    units_in(0, 1)
     finish("q", 2, 1)
     S[7].forward()
+    units_out(0, 1)
     finish("q", 2, 2)
-    pack_rest((4, 5, 6, 7))
-    for g in range(4, 8): S[g].finish()
-    for e in range(2): hidden_units(1, e)
+    pack_rest((5, 6, 7))
+    for g in range(5, 8): S[g].finish()
+    for e in range(2):
+        units_in(1, e)
+        units_out(1, e)
 
     for g in range(8):
         for e in range(2):
@@ -310,7 +315,7 @@
     n0 = (dp * 2).astype(F32)
     line = lax.broadcasted_iota(jnp.int32, (32, 16, 128), 1)
     def routed(k):
-        r = rs[0, :, k * 128:(k + 1) * 128]
+        r = rs[k]
         return (jnp.where(r == n0, spt[0], 0.0) + jnp.where(r == n0 + 1.0, spt[1], 0.0))[:, None, :]
     for k in range(4):
         rr[:, :, k * 128:(k + 1) * 128] = (jnp.where(line == 0, routed(k), 0.0) + jnp.where(line == 1, routed(k + 4), 0.0)).astype(BF)
@@ -321,23 +326,23 @@
     rr_copy.wait()
     for s in pending: s.wait_send()
 
-def experts(hid, gra, ext, wg, wu, wd):
+def experts(hid, gra, routes, probs, wg, wu, wd):
     V=pltpu.VMEM
     A=pl.BlockSpec(memory_space=pl.ANY)
-    N=4 + 3 + 7 + 4 + 2 * (40 + 32) + 64
+    N=7 + 4 + 2 * (40 + 32) + 64
     return pl.pallas_call(expert_kernel,
         out_shape=(jax.ShapeDtypeStruct((2,640,4096),BF), jax.ShapeDtypeStruct((8,160,512),BF), jax.ShapeDtypeStruct((32,16,512),BF), jax.ShapeDtypeStruct((4,4,2,4,128,CQ),BF)),
-        in_specs=[A]*6, out_specs=(A,)*4,
-        scratch_shapes=[V((2,4096,384),BF),V((2,4096,384),BF),V((2,384,4096),BF),
-            V((2,640,4096),BF),V((2,640,4096),BF),V((4,4,2,128,CA),BF),V((4,4,2,16,1024),BF),V((3,32,1024),F32),V((32,16,512),BF),
+        in_specs=[pl.BlockSpec(memory_space=V)]*4+[A]*3, out_specs=(A,)*4,
+        scratch_shapes=[V((2,4096,768),BF),V((2,384,4096),BF),
+            V((2,640,4096),BF),V((2,640,4096),BF),V((4,4,2,128,CA),BF),V((128,CQ),BF),V((4,4,2,32,128),BF),V((24,32,128),F32),V((32,16,512),BF),
             V((8,160,512),BF),V((2,640,128),F32),V((2,640,128),F32),V((4,2,2,128,CQ),BF),
-            V((320,384),F32),V((320,384),F32),V((320,384),F32),V((320,384),BF),V((320,384),BF),V((2,32,128),F32),
+            V((400,768),F32),V((400,384),F32),V((400,768),BF),V((2,32,128),F32),
             pltpu.SemaphoreType.DMA((5,)),pltpu.SemaphoreType.DMA((7,)),pltpu.SemaphoreType.DMA((4,2)),
             pltpu.SemaphoreType.DMA((N,)),pltpu.SemaphoreType.DMA((N,))],
         compiler_params=pltpu.CompilerParams(collective_id=0, has_side_effects=True, vmem_limit_bytes=63*1024*1024),
-    )(hid, gra, ext, wg, wu, wd)[:3]
-
-def return_kernel(ws_hbm, oh_hbm, rr_hbm, pick, grad, router, ws, onehot, rr, y1, y2, red, pq, sq, lq, pa, sa, la, ly, lr, fin, inc,
+    )(hid, gra, routes, probs, wg, wu, wd)[:3]
+
+def return_kernel(ws_hbm, oh_hbm, rr_hbm, partner, swap_count, grad, router, ws, onehot, rr, y1, y2, red, pq, sq, lq, pa, sa, la, ly, lr, fin, inc,
                   in_sem, g_sem, send_sem, recv_sem):
     dp = lax.axis_index("dp"); y = lax.axis_index("tensor")
     x = dp // 8; z = (dp // 2) % 4; c = dp % 2
@@ -477,42 +482,51 @@
         for f in (0, 1): R[q, f, "two"].finish(block(q, f, 0))
 
     for s in small: s.wait()
-    for g in reversed(range(8)):
+    def group(g):
         g_copy(g).wait()
         y_start(g)
         combine_rest(g)
-    for n in range(15, 8, -1): merge("q", n)
-    for s in (2, 1, -1, 0): start_one("q", s)
-    y_middle(7); y_middle(6)
-    for n in range(8, 3, -1): merge("q", n)
-    middle_one("q", 2)
-    y_middle(5); y_middle(4)
-    middle_one("q", 1)
-    for n in range(3, -1, -1): merge("q", n)
-    y_middle(3); y_middle(2)
-    middle_one("q", -1)
-    middle_one("q", 0)
+    def own(*gs):
+        for g in gs:
+            y_finish(g); combine_own(g)
+    def merges(q, *ns):
+        for n in ns: merge(q, n)
+    group(7); group(6)
+    merges("q", 15); start_one("q", 2)
+    group(5)
+    merges("q", 14, 13); start_one("q", 1)
+    group(4)
+    merges("q", 12, 11); start_one("q", -1)
+    y_middle(7); group(3)
+    merges("q", 10, 9); start_one("q", 0)
+    y_middle(6); group(2)
+    merges("q", 8); middle_one("q", 2)
+    y_middle(5); group(1)
+    merges("q", 7, 6); middle_one("q", 1)
+    y_middle(4); group(0)
+    merges("q", 5, 4, 3); middle_one("q", -1)
+    own(7, 6)
+    y_middle(3)
+    merges("q", 2, 1, 0); middle_one("q", 0)
+    y_middle(2)
+    own(5, 4)
+    finish_one("q", 2); start_two("q")
+    merges("a", 15, 14, 13, 12, 11, 10, 9)
+    for s in (2, 1, -1, 0): start_one("a", s)
     y_middle(1); y_middle(0)
-    finish_one("q", 2)
-    start_two("q")
-    for g in (7, 6, 5, 4):
-        y_finish(g); combine_own(g)
-    finish_one("q", 1); finish_one("q", -1)
-    middle_two("q")
-    for g in (3, 2, 1, 0):
-        y_finish(g); combine_own(g)
-    for n in range(15, 8, -1): merge("a", n)
-    for s in (2, 1, -1, 0): start_one("a", s)
+    finish_one("q", 1); finish_one("q", -1); middle_two("q")
+    merges("a", 8); middle_one("a", 2)
+    own(3, 2, 1, 0)
     finish_one("q", 0)
-    for n in range(8, -1, -1): merge("a", n)
-    for s in (2, 1, -1, 0): middle_one("a", s)
+    merges("a", 7, 6); middle_one("a", 1)
+    merges("a", 5, 4, 3); middle_one("a", -1)
+    merges("a", 2, 1, 0); middle_one("a", 0)
+    finish_one("a", 2); start_two("a")
     finish_two("q")
     def rest(k, part=pl.ds(0, 128)):
         return pq.at[c, 0, (y + k + 4) % 4, part]
     lo, hi = pl.ds(0, 64), pl.ds(64, 64)
     last = Ring("y", (ly.at[pl.ds(0, 64)], ly.at[pl.ds(64, 64)], ly.at[pl.ds(128, 128)], ly.at[pl.ds(256, 128)]), rest(2, lo), rest(2, hi))
-    finish_one("a", 2)
-    start_two("a")
     finish_one("a", 1); finish_one("a", -1)
     middle_two("a")
     last.middle(rest(1), rest(1, lo), rest(-1), rest(-1, hi))
@@ -524,24 +538,27 @@
     fin[:, RA:1024] = pq[c, 0, y]
     swaps = [send(fin.at[64:128], inc.at[b], mates[b]) for b in range(3)]
     for o in odds: o.wait_recv()
-    router[...] = (pa[c, 0, 0:16].astype(F32) + lr[0].astype(F32) + lr[1].astype(F32) + lr[2].astype(F32)).astype(BF)
+    total = pa[c, 0, 0:16].astype(F32) + lr[0].astype(F32) + lr[1].astype(F32) + lr[2].astype(F32)
+    table = jnp.concatenate([total[k // 4:k // 4 + 1, (k % 4) * 128:(k % 4 + 1) * 128] for k in range(8)], axis=0)
+    router[...] = table.astype(BF)
     grad[0:64, :] = fin[0:64, :]
     for s in swaps: s.wait_recv()
     row = lax.broadcasted_iota(jnp.int32, (64, 1024), 0)
     kept = fin[64:128, :].astype(F32)
-    taken = row >= 64 - pick[1]
+    taken = row >= 64 - swap_count[dp]
+    apart = jnp.bitwise_xor(partner[dp], dp)
     for b in range(3):
-        kept = jnp.where(taken & (pick[0] == b), inc[b].astype(F32), kept)
+        kept = jnp.where(taken & (apart == (1 << b)), inc[b].astype(F32), kept)
     grad[64:128, :] = kept.astype(BF)
     for s in pending: s.wait_send()
 
-def returned(ws, oh, rr, pick):
+def returned(ws, oh, rr, partner, swap_count):
     V=pltpu.VMEM
     A=pl.BlockSpec(memory_space=pl.ANY)
     N=16 + 16 + 40 + 40 + 32 + 4 + 3 + 3
     return pl.pallas_call(return_kernel,
-        out_shape=(jax.ShapeDtypeStruct((128,1024),BF),jax.ShapeDtypeStruct((16,RA),BF)),
-        in_specs=[A,A,A,pl.BlockSpec(memory_space=pltpu.SMEM)],
+        out_shape=(jax.ShapeDtypeStruct((128,1024),BF),jax.ShapeDtypeStruct((8,128),BF)),
+        in_specs=[A,A,A,pl.BlockSpec(memory_space=pltpu.SMEM),pl.BlockSpec(memory_space=pltpu.SMEM)],
         out_specs=(pl.BlockSpec(memory_space=V),pl.BlockSpec(memory_space=V)),
         scratch_shapes=[V((2,640,4096),BF),V((8,160,512),BF),V((32,16,RA),BF),
             V((8,2,80,RA),BF),V((8,2,2,80,RA),BF),V((8,128),F32),
@@ -550,20 +567,12 @@
             V((384,RQ),BF),V((3,16,RA),BF),V((128,1024),BF),V((3,64,1024),BF),
             pltpu.SemaphoreType.DMA((2,)),pltpu.SemaphoreType.DMA((8,)),pltpu.SemaphoreType.DMA((N,)),pltpu.SemaphoreType.DMA((N,))],
         compiler_params=pltpu.CompilerParams(collective_id=1, has_side_effects=True, vmem_limit_bytes=63*1024*1024),
-    )(ws, oh, rr, pick)
+    )(ws, oh, rr, partner, swap_count)
 
 def local(hidden, grad_out, routes, route_probs, w_gate, w_up, w_down, partner, swap_count):
-    flat = route_probs.T.reshape(1, 1024)
-    high = lax.reduce_precision(flat, 8, 7).astype(BF)
-    low = (flat - high.astype(F32)).astype(BF)
-    number = routes.T.reshape(1, 1024).astype(BF)
-    ext = jnp.concatenate([number, high, low, jnp.zeros((13, 1024), BF)], axis=0)
-    ws, oh, rr = experts(hidden, grad_out, ext, w_gate, w_up, w_down)
-    rank = lax.axis_index("dp")
-    apart = jnp.bitwise_xor(partner[rank], rank)
-    pick = jnp.stack([apart // 2, swap_count[rank]]).astype(jnp.int32)
-    grad, router = returned(ws, oh, rr, pick)
-    return grad, router[:2].reshape(8, 128).T
+    ws, oh, rr = experts(hidden, grad_out, routes.T, route_probs.T, w_gate, w_up, w_down)
+    grad, router = returned(ws, oh, rr, partner, swap_count)
+    return grad, router.T
 
 
 def solution(mesh):

time: 265 us -> 240 us (0.906)
  Pallas kernels: 256 us -> 236 us
  other arithmetic: 3.32 us -> 0 us
    pallas_call x1, Pallas kernels: 170 us -> 159 us  [experts(): pl.pallas_call(expert_kernel, out_shape=(jax.ShapeDtypeStruct((2, 640, 40...]
    pallas_call x1, Pallas kernels: 85.1 us -> 77.7 us  [returned(): pl.pallas_call(return_kernel, out_shape=(jax.ShapeDtypeStruct((128, 1024)...]
where the time goes in v3:
time: 240 us
  Pallas kernels  236 us (98%)
  local copies, waits for them, and re-layouts  2.93 us (1%)
    pallas_call x1, Pallas kernels, experts(): pl.pallas_call(expert_kernel, out_shape=(jax.ShapeDtypeStruct((2, 640, 40...  159 us
    pallas_call x1, Pallas kernels, returned(): pl.pallas_call(return_kernel, out_shape=(jax.ShapeDtypeStruct((128, 1024)...  77.7 us

profile of v3, /device:TPU:0, one launch (start us, length us, event | category | flops | bytes accessed | tf_op | source)
XLA Modules:
  0.0 240.0 jit_solution(16666570090709179569)
XLA Ops:
  0.6 158.7 %shard_map.104 = (bf16[2,640,4096]{2,1,0:T(8,128)(2,1)}, bf16[8,160,512]{2,1,0:T(8,128)(2,1)}, bf16[32,16,512]{2,1,0:T(8,128)(2,1)}, bf16[4,4,2,4,128,896]{5,4,3,2,1,0:T(8,128)(2,1)}) custom-call(bf16[128,1024]{1,0:T(8,128)(2,1)} %hid.1, bf16[128,1024]{1,0:T(8,128)(2,1)} %gra.1, s32[8,128]{1,0:T(8,128)} %bitcast.3, f32[8,128]{1,0:T(8,128)} %bitcast.4, ...), custom_call_target="tpu_custom_call" | custom-call | tf_op jit(solution)/shard_map/pallas_call | solution.py:333
  159.4 77.7 %shard_map.105 = (bf16[128,1024]{1,0:T(8,128)(2,1)}, bf16[8,128]{1,0:T(8,128)(2,1)}) custom-call(bf16[2,640,4096]{2,1,0:T(8,128)(2,1)} %get-tuple-element.7.ws_hbm, bf16[8,160,512]{2,1,0:T(8,128)(2,1)} %get-tuple-element.8.oh_hbm, bf16[32,16,512]{2,1,0:T(8,128)(2,1)} %get-tuple-element.9.rr_hbm, s32[32]{0:T(128)} %partner.1, s32[32]{0:T(128)} %swap_count.1), custom_call_target="tpu_custom_call" | custom-call | tf_op jit(solution)/shard_map/pallas_call | solution.py:559
  237.1 1.7 copy.13
  238.7 1.3 copy.14

commit v4 on v3

--- a/solution.py
+++ b/solution.py
@@ -8,7 +8,7 @@
 
 MESH = pl.DeviceIdType.MESH
 BF=jnp.bfloat16; F32=jnp.float32
-HA=640
+HA=512
 GA=512
 CA=HA+GA
 CQ=2048-CA
@@ -292,14 +292,14 @@
     units_in(0, 0)
     S[5].forward()
     finish("q", 2, -1)
+    forward("q", 2, 2)
     units_out(0, 0)
-    forward("q", 2, 2)
     S[6].forward()
+    finish("q", 2, 1)
     units_in(0, 1)
-    finish("q", 2, 1)
     S[7].forward()
+    finish("q", 2, 2)
     units_out(0, 1)
-    finish("q", 2, 2)
     pack_rest((5, 6, 7))
     for g in range(5, 8): S[g].finish()
     for e in range(2):
@@ -534,9 +534,10 @@
     finish_two("a")
     odds = [send(pa.at[c, 0, pl.ds(0, 16)], lr.at[i], device("y", s)) for i, s in enumerate((1, 2, -1))]
     fin[:, 0:RA] = pa[c, 0, 16:144]
+    swaps = [send(fin.at[64:128, 0:RA], inc.at[b, :, 0:RA], mates[b]) for b in range(3)]
     last.finish(rest(0))
     fin[:, RA:1024] = pq[c, 0, y]
-    swaps = [send(fin.at[64:128], inc.at[b], mates[b]) for b in range(3)]
+    swaps += [send(fin.at[64:128, RA:1024], inc.at[b, :, RA:1024], mates[b]) for b in range(3)]
     for o in odds: o.wait_recv()
     total = pa[c, 0, 0:16].astype(F32) + lr[0].astype(F32) + lr[1].astype(F32) + lr[2].astype(F32)
     table = jnp.concatenate([total[k // 4:k // 4 + 1, (k % 4) * 128:(k % 4 + 1) * 128] for k in range(8)], axis=0)
@@ -555,7 +556,7 @@
 def returned(ws, oh, rr, partner, swap_count):
     V=pltpu.VMEM
     A=pl.BlockSpec(memory_space=pl.ANY)
-    N=16 + 16 + 40 + 40 + 32 + 4 + 3 + 3
+    N=16 + 16 + 40 + 40 + 32 + 4 + 3 + 6
     return pl.pallas_call(return_kernel,
         out_shape=(jax.ShapeDtypeStruct((128,1024),BF),jax.ShapeDtypeStruct((8,128),BF)),
         in_specs=[A,A,A,pl.BlockSpec(memory_space=pltpu.SMEM),pl.BlockSpec(memory_space=pltpu.SMEM)],

time: 240 us -> 236 us (0.983)
  Pallas kernels: 236 us -> 232 us
    pallas_call x1, Pallas kernels: 159 us -> 153 us  [experts(): pl.pallas_call(expert_kernel, out_shape=(jax.ShapeDtypeStruct((2, 640, 40...]
where the time goes in v4:
time: 236 us
  Pallas kernels  232 us (98%)
  local copies, waits for them, and re-layouts  2.93 us (1%)
    pallas_call x1, Pallas kernels, experts(): pl.pallas_call(expert_kernel, out_shape=(jax.ShapeDtypeStruct((2, 640, 40...  153 us
    pallas_call x1, Pallas kernels, returned(): pl.pallas_call(return_kernel, out_shape=(jax.ShapeDtypeStruct((128, 1024)...  79.1 us

profile of v4, /device:TPU:0, one launch (start us, length us, event | category | flops | bytes accessed | tf_op | source)
XLA Modules:
  0.0 235.8 jit_solution(17349886080626219980)
XLA Ops:
  0.6 153.1 %shard_map.104 = (bf16[2,640,4096]{2,1,0:T(8,128)(2,1)}, bf16[8,160,512]{2,1,0:T(8,128)(2,1)}, bf16[32,16,512]{2,1,0:T(8,128)(2,1)}, bf16[4,4,2,4,128,1024]{5,4,3,2,1,0:T(8,128)(2,1)}) custom-call(bf16[128,1024]{1,0:T(8,128)(2,1)} %hid.1, bf16[128,1024]{1,0:T(8,128)(2,1)} %gra.1, s32[8,128]{1,0:T(8,128)} %bitcast.3, f32[8,128]{1,0:T(8,128)} %bitcast.4, ...), custom_call_target="tpu_custom_call" | custom-call | tf_op jit(solution)/shard_map/pallas_call | solution.py:333
  153.7 79.1 %shard_map.105 = (bf16[128,1024]{1,0:T(8,128)(2,1)}, bf16[8,128]{1,0:T(8,128)(2,1)}) custom-call(bf16[2,640,4096]{2,1,0:T(8,128)(2,1)} %get-tuple-element.7.ws_hbm, bf16[8,160,512]{2,1,0:T(8,128)(2,1)} %get-tuple-element.8.oh_hbm, bf16[32,16,512]{2,1,0:T(8,128)(2,1)} %get-tuple-element.9.rr_hbm, s32[32]{0:T(128)} %partner.1, s32[32]{0:T(128)} %swap_count.1), custom_call_target="tpu_custom_call" | custom-call | tf_op jit(solution)/shard_map/pallas_call | solution.py:560
  232.8 1.7 copy.13
  234.5 1.3 copy.14

commit v5 on v4

--- a/solution.py
+++ b/solution.py
@@ -132,6 +132,9 @@
     qy.forward()
     finish("a", 1)
     stage_two("a", (2,))
+    qy.finish()
+    keep.wait()
+    stage_one("q")
     for w in e: w.wait_recv()
     for w in weights: w.start()
 
@@ -162,9 +165,6 @@
             prob[e, g * 80:(g + 1) * 80, :] = jnp.broadcast_to(jnp.sum(oh * w4, axis=1, keepdims=True), (80, 128))
 
     forward("a", 2, 0)
-    qy.finish()
-    keep.wait()
-    stage_one("q")
     waited = set()
     def need(q, g):
         for key in CHIPS[2 * g:2 * g + 2]:
@@ -364,7 +364,7 @@
     for s in small: s.start()
     for g in reversed(range(8)): g_copy(g).start()
     barrier = pltpu.get_barrier_semaphore()
-    partners = [device(a, s) for a in "xyz" for s in (1, -1)] + [device("y", 2)] + mates
+    partners = [device(a, s) for a in "xyz" for s in (1, -1)] + [device("y", 2), device("x", 2)] + mates
     for p in partners:
         pl.semaphore_signal(barrier, inc=1, device_id=p, device_id_type=MESH)
     pl.semaphore_wait(barrier, len(partners))
@@ -481,6 +481,11 @@
     def finish_two(q):
         for f in (0, 1): R[q, f, "two"].finish(block(q, f, 0))
 
+    def direct_land(f, s):
+        return la.at[f, 4, pl.ds(80 * (2, 1, -1).index(s), (80, 64)[f])]
+    def direct(s):
+        for f in (0, 1):
+            R["direct", f, s] = send(block("a", f, chip(f, s, 0)), direct_land(f, s), device("xz"[f], s))
     for s in small: s.wait()
     def group(g):
         g_copy(g).wait()
@@ -521,22 +526,23 @@
     merges("a", 7, 6); middle_one("a", 1)
     merges("a", 5, 4, 3); middle_one("a", -1)
     merges("a", 2, 1, 0); middle_one("a", 0)
-    finish_one("a", 2); start_two("a")
+    finish_one("a", 2); direct(2)
     finish_two("q")
     def rest(k, part=pl.ds(0, 128)):
         return pq.at[c, 0, (y + k + 4) % 4, part]
-    lo, hi = pl.ds(0, 64), pl.ds(64, 64)
-    last = Ring("y", (ly.at[pl.ds(0, 64)], ly.at[pl.ds(64, 64)], ly.at[pl.ds(128, 128)], ly.at[pl.ds(256, 128)]), rest(2, lo), rest(2, hi))
-    finish_one("a", 1); finish_one("a", -1)
-    middle_two("a")
-    last.middle(rest(1), rest(1, lo), rest(-1), rest(-1, hi))
+    last = [send(rest(k), ly.at[pl.ds(128 * i, 128)], device("y", k)) for i, k in enumerate((2, 1, -1))]
+    finish_one("a", 1); direct(1)
+    finish_one("a", -1); direct(-1)
     finish_one("a", 0)
-    finish_two("a")
+    for f in (0, 1):
+        near = block("a", f, 0)
+        for s in (2, 1, -1): R["direct", f, s].wait_recv()
+        add(near, near, *(direct_land(f, s) for s in (2, 1, -1)))
     odds = [send(pa.at[c, 0, pl.ds(0, 16)], lr.at[i], device("y", s)) for i, s in enumerate((1, 2, -1))]
     fin[:, 0:RA] = pa[c, 0, 16:144]
     swaps = [send(fin.at[64:128, 0:RA], inc.at[b, :, 0:RA], mates[b]) for b in range(3)]
-    last.finish(rest(0))
-    fin[:, RA:1024] = pq[c, 0, y]
+    for w in last: w.wait_recv()
+    fin[:, RA:1024] = (pq[c, 0, y].astype(F32) + ly[0:128].astype(F32) + ly[128:256].astype(F32) + ly[256:384].astype(F32)).astype(BF)
     swaps += [send(fin.at[64:128, RA:1024], inc.at[b, :, RA:1024], mates[b]) for b in range(3)]
     for o in odds: o.wait_recv()
     total = pa[c, 0, 0:16].astype(F32) + lr[0].astype(F32) + lr[1].astype(F32) + lr[2].astype(F32)

time: 236 us -> 235 us (level)
  no operation moved by 1% of the time
where the time goes in v5:
time: 235 us; the launch traced here: 234 us
  Pallas kernels  230 us (98%)
  local copies, waits for them, and re-layouts  2.93 us (1%)
    pallas_call x1, Pallas kernels, experts(): pl.pallas_call(expert_kernel, out_shape=(jax.ShapeDtypeStruct((2, 640, 40...  153 us
    pallas_call x1, Pallas kernels, returned(): pl.pallas_call(return_kernel, out_shape=(jax.ShapeDtypeStruct((128, 1024)...  77.3 us

profile of v5, /device:TPU:0, one launch (start us, length us, event | category | flops | bytes accessed | tf_op | source)
XLA Modules:
  0.0 234.0 jit_solution(15671143273897176263)
XLA Ops:
  0.6 153.1 %shard_map.104 = (bf16[2,640,4096]{2,1,0:T(8,128)(2,1)}, bf16[8,160,512]{2,1,0:T(8,128)(2,1)}, bf16[32,16,512]{2,1,0:T(8,128)(2,1)}, bf16[4,4,2,4,128,1024]{5,4,3,2,1,0:T(8,128)(2,1)}) custom-call(bf16[128,1024]{1,0:T(8,128)(2,1)} %hid.1, bf16[128,1024]{1,0:T(8,128)(2,1)} %gra.1, s32[8,128]{1,0:T(8,128)} %bitcast.3, f32[8,128]{1,0:T(8,128)} %bitcast.4, ...), custom_call_target="tpu_custom_call" | custom-call | tf_op jit(solution)/shard_map/pallas_call | solution.py:333
  153.7 77.3 %shard_map.105 = (bf16[128,1024]{1,0:T(8,128)(2,1)}, bf16[8,128]{1,0:T(8,128)(2,1)}) custom-call(bf16[2,640,4096]{2,1,0:T(8,128)(2,1)} %get-tuple-element.7.ws_hbm, bf16[8,160,512]{2,1,0:T(8,128)(2,1)} %get-tuple-element.8.oh_hbm, bf16[32,16,512]{2,1,0:T(8,128)(2,1)} %get-tuple-element.9.rr_hbm, s32[32]{0:T(128)} %partner.1, s32[32]{0:T(128)} %swap_count.1), custom_call_target="tpu_custom_call" | custom-call | tf_op jit(solution)/shard_map/pallas_call | solution.py:566
  231.1 1.7 copy.13
  232.8 1.3 copy.14
